TPU v7x, 128 devices: a whole 4x4x4 slice. The times are simulated.
128 devices in a mesh: row: 8 (over z, core), col: 16 (over x, y).
Axes of the slice: x: 4, y: 4, z: 4, core: 2. Of those that a mesh axis runs over, the one named last changes fastest.
Arguments:
- panel: float32 [2, 16, 1024, 8, 1024], P(None, 'col', None, 'row'), may hold values from -0.03125 to 0.03125
- right_side: float32 [2, 16, 1024, 256], P(None, 'col'), may hold values from -6 to 6
- inverse_blocks: float32 [8, 1024, 1024], P('row'), may hold values from -0.5 to 1.7, as said below
Outputs:
- solved: float32 [8, 1024, 256], P('row')
- updated: float32 [2, 16, 1024, 256], P(None, 'col', 'row')
Inputs may be any that keep to these rules, and one draw needn't show every extreme that they name: `inverse_blocks`: each block is invertible and of order one.
All inputs are finite; a program needn't handle non-finite values.
Results may differ from a plain program's by a relative error of at most 0.0001.
Values sent between devices are 32-bit elements; how exact they have to be, the bound alone decides.
No kernel may reach another device: no remote copies, remote signals or barrier semaphores. Data moves between devices by JAX's collectives and lax.ppermute only.
A program may use at most 128 MiB of HBM per device.

v0:
```python
import jax
import jax.numpy as jnp
from jax import lax
from jax.sharding import PartitionSpec as P


def from_root(array, axis, root):
    mine = lax.axis_index(axis) == root
    return lax.psum(jnp.where(mine, array, jnp.zeros_like(array)), axis)


def shards(panel, right_side, inverse_blocks):
    highest = lax.Precision.HIGHEST
    rows_local = panel.shape[0]
    block = panel.shape[2]
    width = right_side.shape[3]
    tiles = panel.reshape(rows_local, block, block)
    rhs_local = right_side.reshape(rows_local, block, width)
    inverse = inverse_blocks[0]
    my_row = lax.axis_index("row")
    my_col = lax.axis_index("col")
    row_count = lax.axis_size("row")
    col_count = lax.axis_size("col")
    order_ids = jnp.arange(rows_local) * col_count + my_col
    keep = (order_ids > my_row).astype(jnp.float32)[:, None, None]
    empty = jnp.zeros((block, width), jnp.float32)
    partial_value = jnp.zeros((rows_local, block, width), jnp.float32)
    solved = empty
    for k in range(row_count):
        total = lax.psum(partial_value[0], "row")
        local_k = lax.cond(
            my_row == k,
            lambda: jnp.dot(inverse, rhs_local[0] - total, precision=highest),
            lambda: empty,
        )
        solved_k = from_root(local_k, "col", k)
        partial_value = lax.cond(
            my_row == k,
            lambda: keep * jnp.einsum("aij,jn->ain", tiles, solved_k, precision=highest),
            lambda: partial_value,
        )
        solved = jnp.where(my_row == k, solved_k, solved)
    sums = lax.psum_scatter(partial_value, "row", scatter_dimension=1, tiled=True)
    share = block // row_count
    own_rhs = lax.dynamic_slice_in_dim(rhs_local, my_row * share, share, 1)
    updated = (own_rhs - sums).reshape(rows_local, 1, share, width)
    return (solved.reshape(1, block, width), updated)


def solution(mesh):
    placed = (P(None, "col", None, "row", None), P(None, "col", None, None), P("row", None, None))
    return jax.shard_map(
        shards,
        mesh=mesh,
        in_specs=placed,
        out_specs=(P("row", None, None), P(None, "col", "row", None)),
        check_vma=False,
    )
```

profile of v0, /device:TPU:1, one launch (start us, length us, event | category | flops | bytes accessed | tf_op | source)
XLA Modules:
  0.0 1317.2 jit_solution(12367994674201539810)
XLA Ops:
  8.5 8.7 copy.31
  17.3 85.8 %all-reduce.16.cloned.1.call-done = f32[1024,256]{1,0:T(8,128)} async-done(((f32[1024,256]{1,0:T(8,128)}), f32[1024,256]{1,0:T(8,128)}) %all-reduce.16.cloned.1.call-update) | async-done | bytes 1048592 | tf_op jit(solution)/shard_map/psum | solution.py:9
  104.3 68.0 %all-reduce.18.cloned.1.call-done = f32[1024,256]{1,0:T(8,128)} async-done(((f32[1024,256]{1,0:T(8,128)}), f32[1024,256]{1,0:T(8,128)}) %all-reduce.18.cloned.1.call-update) | async-done | bytes 1048592 | tf_op jit(solution)/shard_map/psum | solution.py:30
  172.4 10.9 conditional.18
  172.5 9.4 convolution_bitcast_fusion.1
  181.9 1.3 copy.16
  183.3 1.0 broadcast_select_fusion.6
  184.4 83.6 %all-reduce.20.cloned.1.call-done = f32[1024,256]{1,0:T(8,128)} async-done(((f32[1024,256]{1,0:T(8,128)}), f32[1024,256]{1,0:T(8,128)}) %all-reduce.20.cloned.1.call-update) | async-done | bytes 1048592 | tf_op jit(solution)/shard_map/psum | solution.py:9
  268.0 9.4 conditional.19
  268.0 9.4 convolution_multiply_fusion.1
  278.5 56.7 %all-reduce.22.cloned.1.call-done = f32[1024,256]{1,0:T(8,128)} async-done(((f32[1024,256]{1,0:T(8,128)}), f32[1024,256]{1,0:T(8,128)}) %all-reduce.22.cloned.1.call-update) | async-done | bytes 1048592 | tf_op jit(solution)/shard_map/psum | solution.py:30
  336.3 1.0 broadcast_select_fusion.5
  337.4 94.5 %all-reduce.24.cloned.1.call-done = f32[1024,256]{1,0:T(8,128)} async-done(((f32[1024,256]{1,0:T(8,128)}), f32[1024,256]{1,0:T(8,128)}) %all-reduce.24.cloned.1.call-update) | async-done | bytes 1048592 | tf_op jit(solution)/shard_map/psum | solution.py:9
  433.4 69.3 %all-reduce.26.cloned.1.call-done = f32[1024,256]{1,0:T(8,128)} async-done(((f32[1024,256]{1,0:T(8,128)}), f32[1024,256]{1,0:T(8,128)}) %all-reduce.26.cloned.1.call-update) | async-done | bytes 1048592 | tf_op jit(solution)/shard_map/psum | solution.py:30
  504.8 92.2 %all-reduce.28.cloned.1.call-done = f32[1024,256]{1,0:T(8,128)} async-done(((f32[1024,256]{1,0:T(8,128)}), f32[1024,256]{1,0:T(8,128)}) %all-reduce.28.cloned.1.call-update) | async-done | bytes 1048592 | tf_op jit(solution)/shard_map/psum | solution.py:9
  598.1 67.1 %all-reduce.30.cloned.1.call-done = f32[1024,256]{1,0:T(8,128)} async-done(((f32[1024,256]{1,0:T(8,128)}), f32[1024,256]{1,0:T(8,128)}) %all-reduce.30.cloned.1.call-update) | async-done | bytes 1048592 | tf_op jit(solution)/shard_map/psum | solution.py:30
  665.2 1.2 conditional.24
  666.4 1.1 broadcast_select_fusion.3
  667.5 94.3 %all-reduce.32.cloned.1.call-done = f32[1024,256]{1,0:T(8,128)} async-done(((f32[1024,256]{1,0:T(8,128)}), f32[1024,256]{1,0:T(8,128)}) %all-reduce.32.cloned.1.call-update) | async-done | bytes 1048592 | tf_op jit(solution)/shard_map/psum | solution.py:9
  762.9 70.9 %all-reduce.34.cloned.1.call-done = f32[1024,256]{1,0:T(8,128)} async-done(((f32[1024,256]{1,0:T(8,128)}), f32[1024,256]{1,0:T(8,128)}) %all-reduce.34.cloned.1.call-update) | async-done | bytes 1048592 | tf_op jit(solution)/shard_map/psum | solution.py:30
  835.9 94.3 %all-reduce.36.cloned.1.call-done = f32[1024,256]{1,0:T(8,128)} async-done(((f32[1024,256]{1,0:T(8,128)}), f32[1024,256]{1,0:T(8,128)}) %all-reduce.36.cloned.1.call-update) | async-done | bytes 1048592 | tf_op jit(solution)/shard_map/psum | solution.py:9
  931.5 68.7 %all-reduce.38.cloned.1.call-done = f32[1024,256]{1,0:T(8,128)} async-done(((f32[1024,256]{1,0:T(8,128)}), f32[1024,256]{1,0:T(8,128)}) %all-reduce.38.cloned.1.call-update) | async-done | bytes 1048592 | tf_op jit(solution)/shard_map/psum | solution.py:30
  1001.2 1.0 broadcast_select_fusion.1
  1002.3 95.6 %all-reduce.40.cloned.1.call-done = f32[1024,256]{1,0:T(8,128)} async-done(((f32[1024,256]{1,0:T(8,128)}), f32[1024,256]{1,0:T(8,128)}) %all-reduce.40.cloned.1.call-update) | async-done | bytes 1048592 | tf_op jit(solution)/shard_map/psum | solution.py:9
  1099.1 70.6 %all-reduce.42.cloned.1.call-done = f32[1024,256]{1,0:T(8,128)} async-done(((f32[1024,256]{1,0:T(8,128)}), f32[1024,256]{1,0:T(8,128)}) %all-reduce.42.cloned.1.call-update) | async-done | bytes 1048592 | tf_op jit(solution)/shard_map/psum | solution.py:30
  1169.7 1.3 conditional.30
  1171.0 1.1 broadcast_select_fusion
  1172.1 96.3 %all-reduce.44.cloned.1.call-done = f32[1024,256]{1,0:T(8,128)} async-done(((f32[1024,256]{1,0:T(8,128)}), f32[1024,256]{1,0:T(8,128)}) %all-reduce.44.cloned.1.call-update) | async-done | bytes 1048592 | tf_op jit(solution)/shard_map/psum | solution.py:9
  1268.4 1.3 copy-done
  1270.4 2.7 select_bitcast_fusion
  1273.2 35.3 %reduce-scatter.2.cloned.1.call-done = f32[2,128,256]{2,1,0:T(8,128)} async-done(((f32[2,1024,256]{2,1,0:T(8,128)}), f32[2,128,256]{2,1,0:T(8,128)}) %reduce-scatter.2.cloned.1.call-update) | async-done | bytes 262160 | tf_op jit(solution)/shard_map/reduce_scatter | solution.py:43
  1308.4 1.8 fusion.16
  (67 shorter events, 23.4 us)
Async XLA Ops:
  7.2 95.9 %all-reduce.16.cloned.1.call-start = ((), (), s32[]{:S(2)}) async-start(), calls=%async_computation.1 | async-start | bytes 2097152 | tf_op jit(solution)/shard_map/psum | solution.py:9
  8.5 163.9 %all-reduce.18.cloned.1.call-start = ((), (), s32[]{:S(2)}) async-start(), calls=%async_computation.2 | async-start | bytes 2097152 | tf_op jit(solution)/shard_map/psum | solution.py:30
  104.2 163.7 %all-reduce.20.cloned.1.call-start = ((), (), s32[]{:S(2)}) async-start(), calls=%async_computation.3 | async-start | bytes 2097152 | tf_op jit(solution)/shard_map/psum | solution.py:9
  184.3 150.9 %all-reduce.22.cloned.1.call-start = ((), (), s32[]{:S(2)}) async-start(), calls=%async_computation.4 | async-start | bytes 2097152 | tf_op jit(solution)/shard_map/psum | solution.py:30
  278.4 153.4 %all-reduce.24.cloned.1.call-start = ((), (), s32[]{:S(2)}) async-start(), calls=%async_computation.5 | async-start | bytes 2097152 | tf_op jit(solution)/shard_map/psum | solution.py:9
  337.3 165.3 %all-reduce.26.cloned.1.call-start = ((), (), s32[]{:S(2)}) async-start(), calls=%async_computation.6 | async-start | bytes 2097152 | tf_op jit(solution)/shard_map/psum | solution.py:30
  433.3 163.7 %all-reduce.28.cloned.1.call-start = ((), (), s32[]{:S(2)}) async-start(), calls=%async_computation.7 | async-start | bytes 2097152 | tf_op jit(solution)/shard_map/psum | solution.py:9
  504.7 160.5 %all-reduce.30.cloned.1.call-start = ((), (), s32[]{:S(2)}) async-start(), calls=%async_computation.8 | async-start | bytes 2097152 | tf_op jit(solution)/shard_map/psum | solution.py:30
  598.1 163.7 %all-reduce.32.cloned.1.call-start = ((), (), s32[]{:S(2)}) async-start(), calls=%async_computation.9 | async-start | bytes 2097152 | tf_op jit(solution)/shard_map/psum | solution.py:9
  667.5 166.3 %all-reduce.34.cloned.1.call-start = ((), (), s32[]{:S(2)}) async-start(), calls=%async_computation.10 | async-start | bytes 2097152 | tf_op jit(solution)/shard_map/psum | solution.py:30
  762.8 167.3 %all-reduce.36.cloned.1.call-start = ((), (), s32[]{:S(2)}) async-start(), calls=%async_computation.11 | async-start | bytes 2097152 | tf_op jit(solution)/shard_map/psum | solution.py:9
  835.9 164.3 %all-reduce.38.cloned.1.call-start = ((), (), s32[]{:S(2)}) async-start(), calls=%async_computation.12 | async-start | bytes 2097152 | tf_op jit(solution)/shard_map/psum | solution.py:30
  931.4 166.5 %all-reduce.40.cloned.1.call-start = ((), (), s32[]{:S(2)}) async-start(), calls=%async_computation.13 | async-start | bytes 2097152 | tf_op jit(solution)/shard_map/psum | solution.py:9
  1002.3 167.4 %all-reduce.42.cloned.1.call-start = ((), (), s32[]{:S(2)}) async-start(), calls=%async_computation.14 | async-start | bytes 2097152 | tf_op jit(solution)/shard_map/psum | solution.py:30
  1099.0 169.4 %all-reduce.44.cloned.1.call-start = ((), (), s32[]{:S(2)}) async-start(), calls=%async_computation.15 | async-start | bytes 2097152 | tf_op jit(solution)/shard_map/psum | solution.py:9
  1172.1 136.3 %reduce-scatter.2.cloned.1.call-start = ((), (), s32[]{:S(2)}) async-start(), calls=%async_computation.16 | async-start | bytes 2359296 | tf_op jit(solution)/shard_map/reduce_scatter | solution.py:43
  1268.4 1.4 copy-start
  1268.4 2.0 copy-start.1
Sparse Core Ops, SparseCore 0:
  11.8 91.1 all-reduce.15
  106.0 66.3 all-reduce.17
  184.4 83.5 all-reduce.19
  278.5 56.6 all-reduce.21
  338.9 92.9 all-reduce.23
  434.6 67.9 all-reduce.25
  506.5 90.5 all-reduce.27
  599.9 65.2 all-reduce.29
  669.0 92.7 all-reduce.31
  764.5 69.1 all-reduce.33
  837.6 92.5 all-reduce.35
  933.0 67.1 all-reduce.37
  1004.0 93.9 all-reduce.39
  1100.7 68.9 all-reduce.41
  1173.4 94.9 all-reduce.43
  1270.7 37.6 reduce-scatter.1
where the time goes:
time: 1330 us; the launch traced here: 1320 us
  waiting for transfers between devices  1240 us (93%)
  local copies, waits for them, and re-layouts  25.8 us (2%)
  matrix products  18.7 us (1%)
  between operations  14.6 us (1%)
    psum x8, waiting for transfers between devices, from_root(): return lax.psum(jnp.where(mine, array, jnp.zeros_like(array)), axis)  737 us
    psum x7, waiting for transfers between devices, shards(): total = lax.psum(partial_value[0], 'row')  471 us
    reduce_scatter x1, waiting for transfers between devices, shards(): lax.psum_scatter(partial_value, 'row', scatter_dimension=1, tiled=True)  35.3 us
  transfers between devices with their start and end apart: 16, of which 16 were waited for; matrix products, arithmetic and copies ran while one was open for 1% of the time, Pallas kernels for 0%

commit v1 on v0

v1 whole, which is shorter than its diff:
```python
import functools

import jax
import jax.numpy as jnp
from jax import lax
from jax.experimental import pallas as pl
from jax.experimental.pallas import tpu as pltpu
from jax.sharding import PartitionSpec as P

F32 = jnp.float32
BF16 = jnp.bfloat16
LIMIT = 48 * 1024 * 1024
BOTH = ("row", "col")


def halves(x):
    hi = x.astype(BF16)
    return hi, (x - hi.astype(F32)).astype(BF16)


def joined(x):
    return jnp.concatenate(halves(x), axis=1)


def product(w, cat):
    width = cat.shape[1] // 2
    one = jnp.dot(w[0], cat, preferred_element_type=F32)
    two = jnp.dot(w[1], cat[:, :width], preferred_element_type=F32)
    return one[:, :width] + one[:, width:] + two


def cost(flops, nbytes):
    return pl.CostEstimate(flops=flops, bytes_accessed=nbytes, transcendentals=0)


def params():
    return pltpu.CompilerParams(vmem_limit_bytes=LIMIT)


def place_kernel(core_ref, own_ref, other_ref, out_ref):
    first = core_ref[0] == 0
    own, other = own_ref[...], other_ref[...]
    for slot, value in ((0, jnp.where(first, own, other)), (1, jnp.where(first, other, own))):
        hi, lo = halves(value)
        out_ref[slot, 0] = hi
        out_ref[slot, 1] = lo


def place(core, own, other):
    n, depth = own.shape
    rows = 256
    block = pl.BlockSpec((rows, depth), lambda i, core: (i, 0))
    return pl.pallas_call(
        place_kernel,
        out_shape=jax.ShapeDtypeStruct((2, 2, n, depth), BF16),
        grid_spec=pltpu.PrefetchScalarGridSpec(
            num_scalar_prefetch=1,
            grid=(n // rows,),
            in_specs=[block, block],
            out_specs=pl.BlockSpec((2, 2, rows, depth), lambda i, core: (0, 0, i, 0)),
        ),
        compiler_params=params(),
        cost_estimate=cost(0, 16 * n * depth),
        name="place",
    )(core, own, other)


def weight(slot, first, rows, depth, steps):
    return pl.BlockSpec((None, 2, rows, depth), lambda i: (slot, 0, jnp.clip(i - first, 0, steps - 1), 0))


def whole(shape):
    return pl.BlockSpec(shape, lambda i: (0,) * len(shape))


def first_kernel(steps, rows, wi_ref, wl_ref, r_ref, s_ref, u_ref, cat_ref):
    i = pl.program_id(0)

    @pl.when(i == 0)
    def _():
        cat_ref[...] = joined(r_ref[...])

    @pl.when(i == steps)
    def _():
        cat_ref[...] = joined(s_ref[...])

    @pl.when(i < steps)
    def _():
        s_ref[pl.ds(pl.multiple_of(i * rows, rows), rows), :] = product(wi_ref, cat_ref[...])

    @pl.when(i >= steps)
    def _():
        u_ref[pl.ds(pl.multiple_of((i - steps) * rows, rows), rows), :] = product(wl_ref, cat_ref[...])


def first(wi, wl, r):
    n, width = r.shape
    rows = 256
    steps = n // rows
    out = jax.ShapeDtypeStruct((n, width), F32)
    return pl.pallas_call(
        functools.partial(first_kernel, steps, rows),
        out_shape=(out, out),
        grid=(2 * steps,),
        in_specs=[weight(0, 0, rows, n, steps), weight(0, steps, rows, n, steps), whole((n, width))],
        out_specs=(whole((n, width)), whole((n, width))),
        scratch_shapes=[pltpu.VMEM((n, 2 * width), BF16)],
        compiler_params=params(),
        cost_estimate=cost(12 * n * n * width, 8 * n * n),
        name="first",
    )(wi, wl, r)


def second_kernel(rows, wi_ref, r_ref, u_ref, s_ref, cat_ref):
    i = pl.program_id(0)

    @pl.when(i == 0)
    def _():
        cat_ref[...] = joined(r_ref[...] - u_ref[...])

    s_ref[...] = product(wi_ref, cat_ref[...])


def second(wi, r, u):
    n, width = r.shape
    rows = 256
    steps = n // rows
    return pl.pallas_call(
        functools.partial(second_kernel, rows),
        out_shape=jax.ShapeDtypeStruct((n, width), F32),
        grid=(steps,),
        in_specs=[weight(1, 0, rows, n, steps), whole((n, width)), whole((n, width))],
        out_specs=pl.BlockSpec((rows, width), lambda i: (i, 0)),
        scratch_shapes=[pltpu.VMEM((n, 2 * width), BF16)],
        compiler_params=params(),
        cost_estimate=cost(6 * n * n * width, 4 * n * n),
        name="second",
    )(wi, r, u)


def third_kernel(count, *refs):
    wl_ref, acc_ref, u_ref = refs[:3]
    parts, out_ref, cat_ref = refs[3 : 3 + count], refs[3 + count], refs[4 + count]

    @pl.when(pl.program_id(0) == 0)
    def _():
        cat_ref[...] = joined(sum(p[...] for p in parts))

    out_ref[...] = acc_ref[...] - u_ref[...] - product(wl_ref, cat_ref[...])


def third(wl, acc, u, parts):
    n, width = acc.shape
    rows = 256
    steps = n // rows
    tile = pl.BlockSpec((rows, width), lambda i: (i, 0))
    return pl.pallas_call(
        functools.partial(third_kernel, len(parts)),
        out_shape=jax.ShapeDtypeStruct((n, width), F32),
        grid=(steps,),
        in_specs=[weight(1, 0, rows, n, steps), tile, tile] + [whole((n, width))] * len(parts),
        out_specs=tile,
        scratch_shapes=[pltpu.VMEM((n, 2 * width), BF16)],
        compiler_params=params(),
        cost_estimate=cost(6 * n * n * width, 4 * n * n),
        name="third",
    )(wl, acc, u, *parts)


def update_kernel(keep_ref, w0_ref, w1_ref, s_ref, out_ref, cat_ref):
    @pl.when(pl.program_id(0) == 0)
    def _():
        for slot in range(2):
            cat_ref[slot] = joined(s_ref[slot])

    for a, w_ref in ((0, w0_ref), (1, w1_ref)):
        total = 0.0
        for slot in range(2):
            term = product(w_ref.at[slot], cat_ref[slot])
            total = total + (term * keep_ref[slot] if a == 0 else term)
        out_ref[0, a] = total


def update(keep, w0, w1, s):
    _, n, width = s.shape
    parts = 8
    rows = n // parts
    block = pl.BlockSpec((2, 2, rows, n), lambda i, keep: (0, 0, i, 0))
    return pl.pallas_call(
        update_kernel,
        out_shape=jax.ShapeDtypeStruct((parts, 2, rows, width), F32),
        grid_spec=pltpu.PrefetchScalarGridSpec(
            num_scalar_prefetch=1,
            grid=(parts,),
            in_specs=[block, block, pl.BlockSpec((2, n, width), lambda i, keep: (0, 0, 0))],
            out_specs=pl.BlockSpec((1, 2, rows, width), lambda i, keep: (i, 0, 0, 0)),
            scratch_shapes=[pltpu.VMEM((2, n, 2 * width), BF16)],
        ),
        compiler_params=params(),
        cost_estimate=cost(24 * n * n * width, 16 * n * n),
        name="update",
    )(keep, w0, w1, s)


def shards(panel, right_side, inverse_blocks):
    block = panel.shape[2]
    width = right_side.shape[3] // 2
    my_row, my_col = lax.axis_index("row"), lax.axis_index("col")
    row_count, col_count = lax.axis_size("row"), lax.axis_size("col")
    planes = row_count // 2
    plane, core = my_row // 2, my_row % 2
    core_arg = core.astype(jnp.int32).reshape(1)

    def send(array, moves):
        pairs = [
            ((2 * a + h) * col_count + b, (2 * c + h) * col_count + d)
            for (a, b), (c, d) in moves
            for h in range(2)
        ]
        return lax.ppermute(array, BOTH, pairs)

    def swap(array):
        return lax.ppermute(array, "row", [(r, r ^ 1) for r in range(row_count)])

    tiles = panel.reshape(2, block, block)
    inverse = inverse_blocks[0]
    my_half = lax.dynamic_slice_in_dim(right_side, core * width, width, 3).reshape(2, block, width)
    rhs = my_half[0]

    near = send(rhs, [((0, 0), (0, 1)), ((1, 0), (0, 2)), ((3, 0), (0, 3))])
    far = send(rhs, [((z, 0), (0, 4 + z)) for z in range(4)])
    wi = place(core_arg, inverse, swap(inverse))
    wl = place(core_arg, tiles[0], swap(tiles[0]))
    wl1 = place(core_arg, tiles[1], swap(tiles[1]))

    acc = jnp.where(plane == 0, rhs, jnp.zeros_like(rhs))
    r_p, r_q = near + far, acc
    kept = []
    for m in range(planes):
        low, high = 2 * m, 2 * m + 1
        nxt, last = 2 * m + 2, 2 * m + 3
        s_p, u = first(wi, wl, r_p)
        s_q = second(wi, r_q, u)
        kept.append((s_p, s_q))
        if m == planes - 1:
            break
        to_next = send(s_q, [((m, high), (m, nxt))])
        to_last = send(s_q, [((m, high), (m, last))])
        soon = third(wl, acc, u, [to_next, to_last])
        q_part = send(soon, [((m, nxt), (m + 1, last))])
        other = [((m, last), (m + 1, last))]
        if m < planes - 2:
            other += [((m, nxt), (m + 1, nxt + 2))]
        mixed = send(soon, other)
        is_high = my_col == last
        r_p = q_part
        r_q = mixed
        if m < planes - 2:
            r_p = r_p + jnp.where(is_high, 0.0, mixed)
            r_p = r_p + send(soon, [((m, nxt), (m + 1, nxt + 3))])
            has = jnp.where(my_col == high, s_q, to_next + to_last)
            if m == 0:
                late = [send(has, [((0, 1), (0, 5)), ((0, 2), (0, 6)), ((0, 3), (0, 7))]), send(has, [((0, 1), (0, 4))])]
                r_p = r_p + send(soon, [((0, 2), (1, 6))]) + send(soon, [((0, 2), (1, 7))])
            else:
                late = [send(has, [((1, 3), (1, 7)), ((1, 5), (1, 6))])]
            later = third(wl, acc, u, late)
            moved = send(later, [((m, c), (m + 1, c)) for c in range(nxt + 2, 8)])
            acc = jnp.where(plane == m + 1, moved, acc)

    mine = jnp.stack([sum(s for s, _ in kept), sum(s for _, s in kept)])
    cut = 2 * block // col_count
    pieces = lax.all_to_all(mine.reshape(col_count, cut, width), "col", 0, 0)
    piece = lax.dynamic_index_in_dim(pieces, 2 * plane + 1, 0, keepdims=True)
    pieces = lax.all_to_all(jnp.broadcast_to(piece, pieces.shape), "col", 0, 0)
    mine = pieces.reshape(2, block, width)

    keep = (my_col > 2 * plane + jnp.arange(2)).astype(F32)
    parts = update(keep, wl, wl1, mine)
    parts = lax.all_to_all(parts, "row", 0, 0)
    share = block // row_count
    sums = parts.reshape(planes, 2, 2, share, width).sum(0)
    sums = jnp.concatenate([sums[0], sums[1]], axis=-1)
    own = lax.dynamic_slice_in_dim(right_side, my_row * share, share, 2).reshape(2, share, 2 * width)
    updated = (own - sums).reshape(2, 1, share, 2 * width)

    ours = jnp.where(core == 0, mine[0], mine[1])
    theirs = swap(jnp.where(core == 0, mine[1], mine[0]))
    solved = jnp.concatenate([jnp.where(core == 0, ours, theirs), jnp.where(core == 0, theirs, ours)], axis=1)
    return solved.reshape(1, block, 2 * width), updated


def solution(mesh):
    placed = (P(None, "col", None, "row", None), P(None, "col", None, None), P("row", None, None))
    return jax.shard_map(
        shards,
        mesh=mesh,
        in_specs=placed,
        out_specs=(P("row", None, None), P(None, "col", "row", None)),
        check_vma=False,
    )
```

time: 1330 us -> 301 us (0.23)
  waiting for transfers between devices: 1240 us -> 49.3 us
  starting transfers between devices: 0.65 us -> 117 us
  Pallas kernels: 0 us -> 105 us
  matrix products: 18.7 us -> 0 us
  between operations: 14.6 us -> 1.13 us
    psum x15 -> x0, waiting for transfers between devices: 1210 us -> none  [the longest x8 737 us: from_root(): return lax.psum(jnp.where(mine, array, jnp.zeros_like(array)), axis)]
    pallas_call x0 -> x17, Pallas kernels: none -> 105 us  [the longest x4 31 us: first(): pl.pallas_call(functools.partial(first_kernel, steps, rows), out_shape=(o...]
    all_to_all x0 -> x3, starting transfers between devices: none -> 83.7 us  [the longest x1 66.7 us: shards(): pieces = lax.all_to_all(mine.reshape(col_count, cut, width), 'col', 0, 0)]
    all_to_all x0 -> x3, waiting for transfers between devices: none -> 38.5 us  [the longest x1 17 us: shards(): pieces = lax.all_to_all(mine.reshape(col_count, cut, width), 'col', 0, 0)]
    reduce_scatter x1 -> x0, waiting for transfers between devices: 35.3 us -> none  [shards(): lax.psum_scatter(partial_value, 'row', scatter_dimension=1, tiled=True)]
    ppermute x0 -> x27, starting transfers between devices: none -> 33.7 us  [the longest x23 27.7 us: send(): return lax.ppermute(array, BOTH, pairs)]
    dot_general x2 -> x0, matrix products: 18.7 us -> none  [the longest x1 9.39 us: shards(): jnp.dot(inverse, rhs_local[0] - total, precision=highest)]
  transfers between devices with their start and end apart: 16 -> 30, of which waited for: 16 -> 5; matrix products, arithmetic and copies ran while one was open for 1% -> 4% of each run, Pallas kernels for 0% -> 27%
where the time goes in v1:
time: 301 us; the launch traced here: 299 us
  starting transfers between devices  117 us (39%)
  Pallas kernels  105 us (35%)
  waiting for transfers between devices  49.3 us (16%)
  local copies, waits for them, and re-layouts  15.9 us (5%)
  other arithmetic  10.4 us (3%)
    all_to_all x1, starting transfers between devices, shards(): pieces = lax.all_to_all(mine.reshape(col_count, cut, width), 'col', 0, 0)  66.7 us
    pallas_call x4, Pallas kernels, first(): pl.pallas_call(functools.partial(first_kernel, steps, rows), out_shape=(o...  31 us
    ppermute x23, starting transfers between devices, send(): return lax.ppermute(array, BOTH, pairs)  27.7 us
    pallas_call x5, Pallas kernels, third(): pl.pallas_call(functools.partial(third_kernel, len(parts)), out_shape=jax...  23 us
    pallas_call x3, Pallas kernels, place(): pl.pallas_call(place_kernel, out_shape=jax.ShapeDtypeStruct((2, 2, n, dep...  22.6 us
    all_to_all x1, waiting for transfers between devices, shards(): pieces = lax.all_to_all(mine.reshape(col_count, cut, width), 'col', 0, 0)  17 us
    pallas_call x4, Pallas kernels, second(): pl.pallas_call(functools.partial(second_kernel, rows), out_shape=jax.Shap...  16.4 us
    all_to_all x1, waiting for transfers between devices, shards(): parts = lax.all_to_all(parts, 'row', 0, 0)  14 us
  transfers between devices with their start and end apart: 30, of which 5 were waited for; matrix products, arithmetic and copies ran while one was open for 4% of the time, Pallas kernels for 27%

profile of v1, /device:TPU:1, one launch (start us, length us, event | category | flops | bytes accessed | tf_op | source)
XLA Modules:
  0.0 298.7 jit_solution(15726957476234047867)
XLA Ops:
  0.6 7.9 %fusion = (f32[1,1,1024,1,1024]{4,3,2,1,0:T(1,128)}, f32[1,1,1024,1,1024]{4,3,2,1,0:T(1,128)S(1)}) fusion(f32[2,1,1024,1,1024]{4,3,2,1,0:T(1,128)} %param.3), kind=kLoop, calls=%fused_computation.23 | loop fusion | bytes 16777216 | tf_op jit(solution)/shard_map/slice | solution.py:234
  8.6 3.0 %copy.13 = f32[1,1,1024,1,1024]{4,2,3,1,0:T(8,128)} copy(f32[1,1,1024,1,1024]{4,3,2,1,0:T(1,128)S(1)} %get-tuple-element.21) | data formatting | bytes 8388608
  14.2 3.3 %collective-permute-start.2 = (f32[1024,128]{1,0:T(8,128)S(1)}, f32[1024,128]{1,0:T(8,128)S(1)}, u32[]{:S(2)}, u32[]{:S(2)}) collective-permute-start(f32[1024,128]{1,0:T(8,128)S(1)} %get-tuple-element.19), channel_id=1, source_target_pairs={{0,1},{16,17},{32,2},{48,18},{96,3},{112,19}} | collective-permute-start | bytes 1572872 | tf_op jit(solution)/shard_map/ppermute | solution.py:220
  18.8 9.4 %collective-permute-done.2 = f32[1024,128]{1,0:T(8,128)S(1)} collective-permute-done((f32[1024,128]{1,0:T(8,128)S(1)}, f32[1024,128]{1,0:T(8,128)S(1)}, u32[]{:S(2)}, u32[]{:S(2)}) %collective-permute-start.2) | collective-permute-done | bytes 524320 | tf_op jit(solution)/shard_map/ppermute | solution.py:220
  29.6 7.5 %place.4.wl_ref.refs_0_.w0_ref = bf16[2,2,1024,1024]{3,2,1,0:T(8,128)(2,1)} custom-call(s32[1]{0:T(128)} %bitcast.core_ref, f32[1024,1024]{1,0:T(8,128)} %bitcast.31.own_ref, f32[1024,1024]{1,0:T(8,128)} %collective-permute-done.1.other_ref), custom_call_target="tpu_custom_call" | custom-call | bytes 16777216 | tf_op jit(solution)/shard_map/place/pallas_call | solution.py:53
  37.1 7.5 %place.3.wi_ref = bf16[2,2,1024,1024]{3,2,1,0:T(8,128)(2,1)} custom-call(s32[1]{0:T(128)} %bitcast.core_ref, f32[1024,1024]{1,0:T(8,128)} %bitcast.1.own_ref, f32[1024,1024]{1,0:T(8,128)} %collective-permute-done.other_ref), custom_call_target="tpu_custom_call" | custom-call | bytes 16777216 | tf_op jit(solution)/shard_map/place/pallas_call | solution.py:53
  44.6 7.7 %first.4 = (f32[1024,128]{1,0:T(8,128)S(1)}, f32[1024,128]{1,0:T(8,128)S(1)}) custom-call(bf16[2,2,1024,1024]{3,2,1,0:T(8,128)(2,1)} %place.3.wi_ref, bf16[2,2,1024,1024]{3,2,1,0:T(8,128)(2,1)} %place.4.wl_ref.refs_0_.w0_ref, f32[1024,128]{1,0:T(8,128)S(1)} %add.73.r_ref), custom_call_target="tpu_custom_call" | custom-call | flops 1610612736 | bytes 8388608 | tf_op jit(solution)/shard_map/first/pallas_call | solution.py:101
  52.4 4.2 %second.4 = f32[1024,128]{1,0:T(8,128)S(1)} custom-call(bf16[2,2,1024,1024]{3,2,1,0:T(8,128)(2,1)} %place.3.wi_ref, f32[1024,128]{1,0:T(8,128)S(1)} %get-tuple-element.18.r_ref.refs_1_, f32[1024,128]{1,0:T(8,128)S(1)} %get-tuple-element.11.u_ref.refs_2_), custom_call_target="tpu_custom_call" | custom-call | flops 805306368 | bytes 4194304 | tf_op jit(solution)/shard_map/second/pallas_call | solution.py:128
  58.0 4.8 %third.5 = f32[1024,128]{1,0:T(8,128)} custom-call(bf16[2,2,1024,1024]{3,2,1,0:T(8,128)(2,1)} %place.4.wl_ref.refs_0_.w0_ref, f32[1024,128]{1,0:T(8,128)S(1)} %get-tuple-element.18.r_ref.refs_1_, f32[1024,128]{1,0:T(8,128)S(1)} %get-tuple-element.11.u_ref.refs_2_, f32[1024,128]{1,0:T(8,128)S(1)} %collective-permute-done.4.refs_3_, ...), custom_call_target="tpu_custom_call" | custom-call | flops 805306368 | bytes 4194304 | tf_op jit(solution)/shard_map/third/pallas_call | solution.py:157
  71.0 1.6 add_add_fusion.1.r_ref
  72.6 7.8 %first.5 = (f32[1024,128]{1,0:T(8,128)S(1)}, f32[1024,128]{1,0:T(8,128)S(1)}) custom-call(bf16[2,2,1024,1024]{3,2,1,0:T(8,128)(2,1)} %place.3.wi_ref, bf16[2,2,1024,1024]{3,2,1,0:T(8,128)(2,1)} %place.4.wl_ref.refs_0_.w0_ref, f32[1024,128]{1,0:T(8,128)S(1)} %add_add_fusion.1.r_ref), custom_call_target="tpu_custom_call" | custom-call | flops 1610612736 | bytes 8388608 | tf_op jit(solution)/shard_map/first/pallas_call | solution.py:101
  81.2 4.0 %second.5 = f32[1024,128]{1,0:T(8,128)S(1)} custom-call(bf16[2,2,1024,1024]{3,2,1,0:T(8,128)(2,1)} %place.3.wi_ref, f32[1024,128]{1,0:T(8,128)S(1)} %collective-permute-done.7.r_ref, f32[1024,128]{1,0:T(8,128)S(1)} %get-tuple-element.13.u_ref.refs_2_), custom_call_target="tpu_custom_call" | custom-call | flops 805306368 | bytes 4194304 | tf_op jit(solution)/shard_map/second/pallas_call | solution.py:128
  87.4 4.8 %third.6 = f32[1024,128]{1,0:T(8,128)} custom-call(bf16[2,2,1024,1024]{3,2,1,0:T(8,128)(2,1)} %place.4.wl_ref.refs_0_.w0_ref, f32[1024,128]{1,0:T(8,128)S(1)} %get-tuple-element.18.r_ref.refs_1_, f32[1024,128]{1,0:T(8,128)S(1)} %get-tuple-element.11.u_ref.refs_2_, f32[1024,128]{1,0:T(8,128)S(1)} %collective-permute-done.11.refs_3_, ...), custom_call_target="tpu_custom_call" | custom-call | flops 805306368 | bytes 4194304 | tf_op jit(solution)/shard_map/third/pallas_call | solution.py:157
  93.7 1.9 add_select_fusion
  97.1 4.3 %third.7 = f32[1024,128]{1,0:T(8,128)S(1)} custom-call(bf16[2,2,1024,1024]{3,2,1,0:T(8,128)(2,1)} %place.4.wl_ref.refs_0_.w0_ref, f32[1024,128]{1,0:T(8,128)S(1)} %broadcast_select_fusion.2.refs_1_, f32[1024,128]{1,0:T(8,128)S(1)} %get-tuple-element.13.u_ref.refs_2_, f32[1024,128]{1,0:T(8,128)S(1)} %collective-permute-done.14.refs_3_, ...), custom_call_target="tpu_custom_call" | custom-call | flops 805306368 | bytes 4194304 | tf_op jit(solution)/shard_map/third/pallas_call | solution.py:157
  105.0 3.0 copy.12
  109.4 4.9 %third.8 = f32[1024,128]{1,0:T(8,128)} custom-call(bf16[2,2,1024,1024]{3,2,1,0:T(8,128)(2,1)} %place.4.wl_ref.refs_0_.w0_ref, f32[1024,128]{1,0:T(8,128)S(1)} %broadcast_select_fusion.2.refs_1_, f32[1024,128]{1,0:T(8,128)S(1)} %get-tuple-element.13.u_ref.refs_2_, f32[1024,128]{1,0:T(8,128)} %collective-permute-done.19.refs_3_), custom_call_target="tpu_custom_call" | custom-call | flops 805306368 | bytes 4194304 | tf_op jit(solution)/shard_map/third/pallas_call | solution.py:157
  117.0 7.8 %first.6 = (f32[1024,128]{1,0:T(8,128)S(1)}, f32[1024,128]{1,0:T(8,128)S(1)}) custom-call(bf16[2,2,1024,1024]{3,2,1,0:T(8,128)(2,1)} %place.3.wi_ref, bf16[2,2,1024,1024]{3,2,1,0:T(8,128)(2,1)} %place.4.wl_ref.refs_0_.w0_ref, f32[1024,128]{1,0:T(8,128)S(1)} %add_add_fusion.r_ref), custom_call_target="tpu_custom_call" | custom-call | flops 1610612736 | bytes 8388608 | tf_op jit(solution)/shard_map/first/pallas_call | solution.py:101
  124.8 4.2 %second.6 = f32[1024,128]{1,0:T(8,128)S(1)} custom-call(bf16[2,2,1024,1024]{3,2,1,0:T(8,128)(2,1)} %place.3.wi_ref, f32[1024,128]{1,0:T(8,128)S(1)} %collective-permute-done.17.r_ref, f32[1024,128]{1,0:T(8,128)S(1)} %get-tuple-element.15.u_ref.refs_2_), custom_call_target="tpu_custom_call" | custom-call | flops 805306368 | bytes 4194304 | tf_op jit(solution)/shard_map/second/pallas_call | solution.py:128
  131.2 4.1 %third.9 = f32[1024,128]{1,0:T(8,128)S(1)} custom-call(bf16[2,2,1024,1024]{3,2,1,0:T(8,128)(2,1)} %place.4.wl_ref.refs_0_.w0_ref, f32[1024,128]{1,0:T(8,128)S(1)} %broadcast_select_fusion.1.refs_1_, f32[1024,128]{1,0:T(8,128)S(1)} %get-tuple-element.15.u_ref.refs_2_, f32[1024,128]{1,0:T(8,128)S(1)} %collective-permute-done.21.refs_3_, ...), custom_call_target="tpu_custom_call" | custom-call | flops 805306368 | bytes 4194304 | tf_op jit(solution)/shard_map/third/pallas_call | solution.py:157
  136.8 7.8 %first.7 = (f32[1024,128]{1,0:T(8,128)S(1)}, f32[1024,128]{1,0:T(8,128)S(1)}) custom-call(bf16[2,2,1024,1024]{3,2,1,0:T(8,128)(2,1)} %place.3.wi_ref, bf16[2,2,1024,1024]{3,2,1,0:T(8,128)(2,1)} %place.4.wl_ref.refs_0_.w0_ref, f32[1024,128]{1,0:T(8,128)S(1)} %collective-permute-done.23.r_ref), custom_call_target="tpu_custom_call" | custom-call | flops 1610612736 | bytes 8388608 | tf_op jit(solution)/shard_map/first/pallas_call | solution.py:101
  144.6 4.1 %second.7 = f32[1024,128]{1,0:T(8,128)S(1)} custom-call(bf16[2,2,1024,1024]{3,2,1,0:T(8,128)(2,1)} %place.3.wi_ref, f32[1024,128]{1,0:T(8,128)S(1)} %collective-permute-done.24.r_ref, f32[1024,128]{1,0:T(8,128)S(1)} %get-tuple-element.17.u_ref), custom_call_target="tpu_custom_call" | custom-call | flops 805306368 | bytes 4194304 | tf_op jit(solution)/shard_map/second/pallas_call | solution.py:128
  150.0 66.7 %all-to-all-start = ((f32[16,128,128]{2,1,0:T(8,128)}), f32[16,128,128]{2,1,0:T(8,128)S(1)}, u32[]{:S(2)}, u32[]{:S(2)}) async-start(f32[16,128,128]{2,1,0:T(8,128)} %bitcast.6), calls=%async_computation | async-start | bytes 2097152 | tf_op jit(solution)/shard_map/all_to_all | solution.py:273
  216.7 17.0 %all-to-all-done = f32[16,128,128]{2,1,0:T(8,128)S(1)} async-done(((f32[16,128,128]{2,1,0:T(8,128)}), f32[16,128,128]{2,1,0:T(8,128)S(1)}, u32[]{:S(2)}, u32[]{:S(2)}) %all-to-all-start) | async-done | bytes 1048608 | tf_op jit(solution)/shard_map/all_to_all | solution.py:273
  234.8 3.7 %all-to-all-start.1 = ((f32[16,128,128]{2,1,0:T(8,128)}), f32[16,128,128]{2,1,0:T(8,128)S(1)}, u32[]{:S(2)}, u32[]{:S(2)}) async-start(f32[16,128,128]{2,1,0:T(8,128)} %broadcast_in_dim.15), calls=%async_computation.1 | async-start | bytes 2097152 | tf_op jit(solution)/shard_map/all_to_all | solution.py:275
  238.4 7.5 %place.5.w1_ref = bf16[2,2,1024,1024]{3,2,1,0:T(8,128)(2,1)} custom-call(s32[1]{0:T(128)} %bitcast.core_ref, f32[1024,1024]{1,0:T(8,128)} %bitcast.30.own_ref, f32[1024,1024]{1,0:T(8,128)} %collective-permute-done.26.other_ref), custom_call_target="tpu_custom_call" | custom-call | bytes 16777216 | tf_op jit(solution)/shard_map/place/pallas_call | solution.py:53
  246.0 7.5 %all-to-all-done.1 = f32[16,128,128]{2,1,0:T(8,128)S(1)} async-done(((f32[16,128,128]{2,1,0:T(8,128)}), f32[16,128,128]{2,1,0:T(8,128)S(1)}, u32[]{:S(2)}, u32[]{:S(2)}) %all-to-all-start.1) | async-done | bytes 1048608 | tf_op jit(solution)/shard_map/all_to_all | solution.py:275
  253.6 3.2 %collective-permute-start.25 = (f32[1024,128]{1,0:T(8,128)S(1)}, f32[1024,128]{1,0:T(8,128)S(1)}, u32[]{:S(2)}, u32[]{:S(2)}) collective-permute-start(f32[1024,128]{1,0:T(8,128)S(1)} %bitcast.34), channel_id=1, source_target_pairs={{0,16},{16,0},{32,48},{48,32},{64,80},{80,64},{96,112},{112,96},{1... | collective-permute-start | bytes 1572872 | tf_op jit(solution)/shard_map/ppermute | solution.py:223
  256.8 11.7 %update.1 = f32[8,2,128,128]{3,2,1,0:T(8,128)} custom-call(f32[2]{0:T(128)S(1)} %compare_convert_fusion.keep_ref, bf16[2,2,1024,1024]{3,2,1,0:T(8,128)(2,1)} %place.4.wl_ref.refs_0_.w0_ref, bf16[2,2,1024,1024]{3,2,1,0:T(8,128)(2,1)} %place.5.w1_ref, f32[2,1024,128]{2,1,0:T(8,128)S(1)} %bitcast.32), custom_call_target="tpu_custom_call" | custom-call | flops 3221225472 | bytes 16777216 | tf_op jit(solution)/shard_map/update/pallas_call | solution.py:189
  268.5 13.3 %all-to-all-start.2 = ((f32[8,2,128,128]{3,2,1,0:T(8,128)}), f32[8,2,128,128]{3,2,1,0:T(8,128)S(1)}, u32[]{:S(2)}, u32[]{:S(2)}) async-start(f32[8,2,128,128]{3,2,1,0:T(8,128)} %update.1), calls=%async_computation.2 | async-start | bytes 2097152 | tf_op jit(solution)/shard_map/all_to_all | solution.py:280
  283.0 14.0 %all-to-all-done.2 = f32[8,2,128,128]{3,2,1,0:T(8,128)S(1)} async-done(((f32[8,2,128,128]{3,2,1,0:T(8,128)}), f32[8,2,128,128]{3,2,1,0:T(8,128)S(1)}, u32[]{:S(2)}, u32[]{:S(2)}) %all-to-all-start.2) | async-done | bytes 1048608 | tf_op jit(solution)/shard_map/all_to_all | solution.py:280
  297.0 1.7 maximum_subtract_fusion
  (82 shorter events, 35.6 us)
Async XLA Ops:
  11.6 18.0 %collective-permute-start.1 = (f32[1024,1024]{1,0:T(8,128)}, f32[1024,1024]{1,0:T(8,128)}, u32[]{:S(2)}, u32[]{:S(2)}) collective-permute-start(f32[1024,1024]{1,0:T(8,128)} %bitcast.31.own_ref), channel_id=1, source_target_pairs={{0,16},{16,0},{32,48},{48,32},{64,80},{80,64},{96,112},{112,96},{1... | collective-permute-start | bytes 12582920 | tf_op jit(solution)/shard_map/ppermute | solution.py:223
  13.0 24.1 %collective-permute-start = (f32[1024,1024]{1,0:T(8,128)}, f32[1024,1024]{1,0:T(8,128)}, u32[]{:S(2)}, u32[]{:S(2)}) collective-permute-start(f32[1024,1024]{1,0:T(8,128)} %bitcast.1.own_ref), channel_id=1, source_target_pairs={{0,16},{16,0},{32,48},{48,32},{64,80},{80,64},{96,112},{112,96},{1... | collective-permute-start | bytes 12582920 | tf_op jit(solution)/shard_map/ppermute | solution.py:223
  14.2 14.1 %collective-permute-start.2 = (f32[1024,128]{1,0:T(8,128)S(1)}, f32[1024,128]{1,0:T(8,128)S(1)}, u32[]{:S(2)}, u32[]{:S(2)}) collective-permute-start(f32[1024,128]{1,0:T(8,128)S(1)} %get-tuple-element.19), channel_id=1, source_target_pairs={{0,1},{16,17},{32,2},{48,18},{96,3},{112,19}} | collective-permute-start | bytes 1572872 | tf_op jit(solution)/shard_map/ppermute | solution.py:220
  17.5 12.1 %collective-permute-start.3 = (f32[1024,128]{1,0:T(8,128)S(1)}, f32[1024,128]{1,0:T(8,128)S(1)}, u32[]{:S(2)}, u32[]{:S(2)}) collective-permute-start(f32[1024,128]{1,0:T(8,128)S(1)} %get-tuple-element.19), channel_id=1, source_target_pairs={{0,4},{16,20},{32,5},{48,21},{64,6},{80,22},{96,7},{112,23}} | collective-permute-start | bytes 1572872 | tf_op jit(solution)/shard_map/ppermute | solution.py:220
  56.6 1.4 collective-permute-start.4
  57.3 0.7 collective-permute-start.5
  62.9 6.7 %collective-permute-start.10 = (f32[1024,128]{1,0:T(8,128)}, f32[1024,128]{1,0:T(8,128)}, u32[]{:S(2)}, u32[]{:S(2)}) collective-permute-start(f32[1024,128]{1,0:T(8,128)} %third.5), channel_id=1, source_target_pairs={{2,39},{18,55}} | collective-permute-start | bytes 1572872 | tf_op jit(solution)/shard_map/ppermute | solution.py:220
  64.3 5.9 %collective-permute-start.6 = (f32[1024,128]{1,0:T(8,128)}, f32[1024,128]{1,0:T(8,128)}, u32[]{:S(2)}, u32[]{:S(2)}) collective-permute-start(f32[1024,128]{1,0:T(8,128)} %third.5), channel_id=1, source_target_pairs={{2,35},{18,51}} | collective-permute-start | bytes 1572872 | tf_op jit(solution)/shard_map/ppermute | solution.py:220
  65.8 5.2 %collective-permute-start.7 = (f32[1024,128]{1,0:T(8,128)}, f32[1024,128]{1,0:T(8,128)S(1)}, u32[]{:S(2)}, u32[]{:S(2)}) collective-permute-start(f32[1024,128]{1,0:T(8,128)} %third.5), channel_id=1, source_target_pairs={{3,35},{19,51},{2,36},{18,52}} | collective-permute-start | bytes 1572872 | tf_op jit(solution)/shard_map/ppermute | solution.py:220
  66.5 4.5 %collective-permute-start.8 = (f32[1024,128]{1,0:T(8,128)}, f32[1024,128]{1,0:T(8,128)}, u32[]{:S(2)}, u32[]{:S(2)}) collective-permute-start(f32[1024,128]{1,0:T(8,128)} %third.5), channel_id=1, source_target_pairs={{2,37},{18,53}} | collective-permute-start | bytes 1572872 | tf_op jit(solution)/shard_map/ppermute | solution.py:220
  67.9 3.0 %collective-permute-start.9 = (f32[1024,128]{1,0:T(8,128)}, f32[1024,128]{1,0:T(8,128)}, u32[]{:S(2)}, u32[]{:S(2)}) collective-permute-start(f32[1024,128]{1,0:T(8,128)} %third.5), channel_id=1, source_target_pairs={{2,38},{18,54}} | collective-permute-start | bytes 1572872 | tf_op jit(solution)/shard_map/ppermute | solution.py:220
  69.5 17.8 %collective-permute-start.11 = (f32[1024,128]{1,0:T(8,128)S(1)}, f32[1024,128]{1,0:T(8,128)S(1)}, u32[]{:S(2)}, u32[]{:S(2)}) collective-permute-start(f32[1024,128]{1,0:T(8,128)S(1)} %add_select_fusion.1), channel_id=1, source_target_pairs={{1,5},{17,21},{2,6},{18,22},{3,7},{19,23}} | collective-permute-start | bytes 1572872 | tf_op jit(solution)/shard_map/ppermute | solution.py:220
  70.2 17.1 %collective-permute-start.12 = (f32[1024,128]{1,0:T(8,128)S(1)}, f32[1024,128]{1,0:T(8,128)S(1)}, u32[]{:S(2)}, u32[]{:S(2)}) collective-permute-start(f32[1024,128]{1,0:T(8,128)S(1)} %add_select_fusion.1), channel_id=1, source_target_pairs={{1,4},{17,20}} | collective-permute-start | bytes 1572872 | tf_op jit(solution)/shard_map/ppermute | solution.py:220
  85.2 8.5 %collective-permute-start.14 = (f32[1024,128]{1,0:T(8,128)S(1)}, f32[1024,128]{1,0:T(8,128)S(1)}, u32[]{:S(2)}, u32[]{:S(2)}) collective-permute-start(f32[1024,128]{1,0:T(8,128)S(1)} %second.5), channel_id=1, source_target_pairs={{35,36},{51,52}} | collective-permute-start | bytes 1572872 | tf_op jit(solution)/shard_map/ppermute | solution.py:220
  85.9 7.8 %collective-permute-start.15 = (f32[1024,128]{1,0:T(8,128)S(1)}, f32[1024,128]{1,0:T(8,128)}, u32[]{:S(2)}, u32[]{:S(2)}) collective-permute-start(f32[1024,128]{1,0:T(8,128)S(1)} %second.5), channel_id=1, source_target_pairs={{35,37},{51,53}} | collective-permute-start | bytes 1572872 | tf_op jit(solution)/shard_map/ppermute | solution.py:220
  92.2 4.9 %collective-permute-start.13 = (f32[1024,128]{1,0:T(8,128)}, f32[1024,128]{1,0:T(8,128)}, u32[]{:S(2)}, u32[]{:S(2)}) collective-permute-start(f32[1024,128]{1,0:T(8,128)} %third.6), channel_id=1, source_target_pairs={{4,36},{20,52},{5,37},{21,53},{6,38},{22,54},{7,39},{23,55}} | collective-permute-start | bytes 1572872 | tf_op jit(solution)/shard_map/ppermute | solution.py:220
  95.6 13.8 %collective-permute-start.19 = (f32[1024,128]{1,0:T(8,128)}, f32[1024,128]{1,0:T(8,128)}, u32[]{:S(2)}, u32[]{:S(2)}) collective-permute-start(f32[1024,128]{1,0:T(8,128)} %add_select_fusion), channel_id=1, source_target_pairs={{35,39},{51,55},{37,38},{53,54}} | collective-permute-start | bytes 1572872 | tf_op jit(solution)/shard_map/ppermute | solution.py:220
  97.1 7.9 %copy-start.6 = (f32[1,1,1024,1,1024]{4,3,2,1,0:T(1,128)S(1)}, f32[1,1,1024,1,1024]{4,3,2,1,0:T(1,128)}, u32[]{:S(2)}) copy-start(f32[1,1,1024,1,1024]{4,3,2,1,0:T(1,128)} %get-tuple-element.20) | copy-start | bytes 12582916
  101.4 14.3 %collective-permute-start.16 = (f32[1024,128]{1,0:T(8,128)S(1)}, f32[1024,128]{1,0:T(8,128)}, u32[]{:S(2)}, u32[]{:S(2)}) collective-permute-start(f32[1024,128]{1,0:T(8,128)S(1)} %third.7), channel_id=1, source_target_pairs={{36,69},{52,85}} | collective-permute-start | bytes 1572872 | tf_op jit(solution)/shard_map/ppermute | solution.py:220
  102.9 12.8 %collective-permute-start.17 = (f32[1024,128]{1,0:T(8,128)S(1)}, f32[1024,128]{1,0:T(8,128)S(1)}, u32[]{:S(2)}, u32[]{:S(2)}) collective-permute-start(f32[1024,128]{1,0:T(8,128)S(1)} %third.7), channel_id=1, source_target_pairs={{37,69},{53,85},{36,70},{52,86}} | collective-permute-start | bytes 1572872 | tf_op jit(solution)/shard_map/ppermute | solution.py:220
  103.6 12.2 %collective-permute-start.18 = (f32[1024,128]{1,0:T(8,128)S(1)}, f32[1024,128]{1,0:T(8,128)}, u32[]{:S(2)}, u32[]{:S(2)}) collective-permute-start(f32[1024,128]{1,0:T(8,128)S(1)} %third.7), channel_id=1, source_target_pairs={{36,71},{52,87}} | collective-permute-start | bytes 1572872 | tf_op jit(solution)/shard_map/ppermute | solution.py:220
  108.0 130.4 %collective-permute-start.26 = (f32[1024,1024]{1,0:T(8,128)}, f32[1024,1024]{1,0:T(8,128)}, u32[]{:S(2)}, u32[]{:S(2)}) collective-permute-start(f32[1024,1024]{1,0:T(8,128)} %bitcast.30.own_ref), channel_id=1, source_target_pairs={{0,16},{16,0},{32,48},{48,32},{64,80},{80,64},{96,112},{112,96},{1... | collective-permute-start | bytes 12582920 | tf_op jit(solution)/shard_map/ppermute | solution.py:223
  114.3 16.9 %collective-permute-start.20 = (f32[1024,128]{1,0:T(8,128)}, f32[1024,128]{1,0:T(8,128)}, u32[]{:S(2)}, u32[]{:S(2)}) collective-permute-start(f32[1024,128]{1,0:T(8,128)} %third.8), channel_id=1, source_target_pairs={{38,70},{54,86},{39,71},{55,87}} | collective-permute-start | bytes 1572872 | tf_op jit(solution)/shard_map/ppermute | solution.py:220
  129.0 2.2 collective-permute-start.21
  129.7 1.5 collective-permute-start.22
  135.4 1.4 collective-permute-start.23
  136.1 8.5 %collective-permute-start.24 = (f32[1024,128]{1,0:T(8,128)S(1)}, f32[1024,128]{1,0:T(8,128)S(1)}, u32[]{:S(2)}, u32[]{:S(2)}) collective-permute-start(f32[1024,128]{1,0:T(8,128)S(1)} %third.9), channel_id=1, source_target_pairs={{71,103},{87,119}} | collective-permute-start | bytes 1572872 | tf_op jit(solution)/shard_map/ppermute | solution.py:220
  144.6 4.2 %copy-start.1 = (f32[1024,128]{1,0:T(8,128)S(1)}, f32[1024,128]{1,0:T(8,128)}, u32[]{:S(2)}) copy-start(f32[1024,128]{1,0:T(8,128)} %copy-done) | copy-start | bytes 1572868
  150.0 83.7 %all-to-all-start = ((f32[16,128,128]{2,1,0:T(8,128)}), f32[16,128,128]{2,1,0:T(8,128)S(1)}, u32[]{:S(2)}, u32[]{:S(2)}) async-start(f32[16,128,128]{2,1,0:T(8,128)} %bitcast.6), calls=%async_computation | async-start | bytes 2097152 | tf_op jit(solution)/shard_map/all_to_all | solution.py:273
  234.8 18.7 %all-to-all-start.1 = ((f32[16,128,128]{2,1,0:T(8,128)}), f32[16,128,128]{2,1,0:T(8,128)S(1)}, u32[]{:S(2)}, u32[]{:S(2)}) async-start(f32[16,128,128]{2,1,0:T(8,128)} %broadcast_in_dim.15), calls=%async_computation.1 | async-start | bytes 2097152 | tf_op jit(solution)/shard_map/all_to_all | solution.py:275
  253.6 28.3 %collective-permute-start.25 = (f32[1024,128]{1,0:T(8,128)S(1)}, f32[1024,128]{1,0:T(8,128)S(1)}, u32[]{:S(2)}, u32[]{:S(2)}) collective-permute-start(f32[1024,128]{1,0:T(8,128)S(1)} %bitcast.34), channel_id=1, source_target_pairs={{0,16},{16,0},{32,48},{48,32},{64,80},{80,64},{96,112},{112,96},{1... | collective-permute-start | bytes 1572872 | tf_op jit(solution)/shard_map/ppermute | solution.py:223
  268.5 28.4 %all-to-all-start.2 = ((f32[8,2,128,128]{3,2,1,0:T(8,128)}), f32[8,2,128,128]{3,2,1,0:T(8,128)S(1)}, u32[]{:S(2)}, u32[]{:S(2)}) async-start(f32[8,2,128,128]{3,2,1,0:T(8,128)} %update.1), calls=%async_computation.2 | async-start | bytes 2097152 | tf_op jit(solution)/shard_map/all_to_all | solution.py:280
  (5 other events, 17.7 us)

commit v2 on v0

v2 whole, which is shorter than its diff:
```python
import functools

import jax
import jax.numpy as jnp
from jax import lax
from jax.experimental import pallas as pl
from jax.experimental.pallas import tpu as pltpu
from jax.sharding import PartitionSpec as P

F32 = jnp.float32
BF16 = jnp.bfloat16
LIMIT = 16 * 1024 * 1024
BOTH = ("row", "col")
VMEM = pl.BlockSpec(memory_space=pltpu.VMEM)
SMEM = pl.BlockSpec(memory_space=pltpu.SMEM)
ANY = pl.BlockSpec(memory_space=pl.ANY)


def halves(x):
    hi = x.astype(BF16)
    return hi, (x - hi.astype(F32)).astype(BF16)


def joined(x):
    return jnp.concatenate(halves(x), axis=1)


def product(w, cat):
    width = cat.shape[1] // 2
    one = jnp.dot(w[0], cat, preferred_element_type=F32)
    two = jnp.dot(w[1], cat[:, :width], preferred_element_type=F32)
    return one[:, :width] + one[:, width:] + two


def packed(x, half):
    n, width = x.shape
    part = x[:, half * width // 2 : (half + 1) * width // 2]
    return jnp.concatenate([part[: n // 2], part[n // 2 :]], axis=1)


def unpacked(x):
    width = x.shape[1] // 2
    return jnp.concatenate([x[:, :width], x[:, width:]], axis=0)


def cost(flops, nbytes):
    return pl.CostEstimate(flops=1, bytes_accessed=1, transcendentals=0)


def call(kernel, name, products, outs, specs, *args):
    n = 1024
    return pl.pallas_call(
        kernel,
        out_shape=tuple(jax.ShapeDtypeStruct(shape, kind) for shape, kind in outs),
        in_specs=specs,
        out_specs=(VMEM,) * len(outs),
        compiler_params=pltpu.CompilerParams(vmem_limit_bytes=LIMIT),
        cost_estimate=cost(6 * products * n * n * 128, 4 * products * n * n),
        name=name,
    )(*args)


def after(x, *others):
    return lax.optimization_barrier((x,) + others)[0]


def retile_kernel(a, panel_ref, out_ref, sem):
    copy = pltpu.make_async_copy(panel_ref.at[a, 0, :, 0], out_ref, sem.at[0])
    copy.start()
    copy.wait()


def retile(panel, a):
    n, depth = panel.shape[2], panel.shape[4]
    return pl.pallas_call(
        functools.partial(retile_kernel, a),
        out_shape=jax.ShapeDtypeStruct((n, depth), F32),
        in_specs=[pl.BlockSpec(memory_space=pltpu.HBM)],
        out_specs=VMEM,
        scratch_shapes=[pltpu.SemaphoreType.DMA((1,))],
        compiler_params=pltpu.CompilerParams(vmem_limit_bytes=(56 - 40 * a) * 1024 * 1024),
        cost_estimate=cost(0, 8 * n * depth),
        name="retile",
    )(panel)


def place_kernel(core_ref, own_ref, other_ref, out_ref, *ahead):
    core = core_ref[0]
    for slot, ref in ((core, own_ref), (1 - core, other_ref)):
        hi, lo = halves(ref[...])
        out_ref[slot, 0] = hi
        out_ref[slot, 1] = lo
    step = pl.program_id(0)
    rows = own_ref.shape[0]
    for ahead_ref in ahead:
        for h, ref in ((0, own_ref), (1, other_ref)):

            @pl.when((core == h) & (step // 2 == h))
            def _():
                ahead_ref[pl.ds(pl.multiple_of((step - 2 * h) * rows, rows), rows), :] = ref[...]


def place(core, own, other, ahead):
    n, depth = own.shape
    rows = n // 4
    block = pl.BlockSpec((rows, depth), lambda i, core: (i, 0))
    still = pl.BlockSpec((n // 2, depth), lambda i, core: (0, 0))
    return pl.pallas_call(
        place_kernel,
        out_shape=[jax.ShapeDtypeStruct((2, 2, n, depth), BF16)] + [jax.ShapeDtypeStruct((n // 2, depth), F32)] * ahead,
        grid_spec=pltpu.PrefetchScalarGridSpec(
            num_scalar_prefetch=1,
            grid=(4,),
            in_specs=[block, block],
            out_specs=[pl.BlockSpec((2, 2, rows, depth), lambda i, core: (0, 0, i, 0))] + [still] * ahead,
        ),
        compiler_params=pltpu.CompilerParams(vmem_limit_bytes=LIMIT),
        cost_estimate=cost(0, 16 * n * depth),
        name="place",
    )(core, own, other)


def first_kernel(wi_ref, wl_ref, flag_ref, a_ref, b_ref, c_ref, s_ref, u_ref):
    r = a_ref[...] + c_ref[...] + b_ref[...] * flag_ref[0].astype(F32)
    s = product(wi_ref.at[0], joined(r))
    s_ref[...] = s
    u_ref[...] = product(wl_ref.at[0], joined(s))


def second_kernel(wi_ref, r_ref, u_ref, s_ref):
    s_ref[...] = product(wi_ref.at[1], joined(r_ref[...] - u_ref[...]))


def third_kernel(wl_ref, acc_ref, u_ref, *refs):
    parts, out_ref, sum_ref = refs[:-2], refs[-2], refs[-1]
    s = functools.reduce(jnp.add, [p[...] for p in parts])
    sum_ref[...] = s
    out_ref[...] = acc_ref[...] - u_ref[...] - product(wl_ref.at[1], joined(s))


def both_ways(even, x, one_ref, two_ref):
    low, high = packed(x, 0), packed(x, 1)
    one_ref[...] = jnp.where(even, low, high)
    two_ref[...] = jnp.where(even, high, low)


def pair_kernel(wi_ref, wl_ref, wq_ref, even_ref, a_ref, b_ref, one_ref, two_ref, p_ref, q_ref):
    even = even_ref[0] == 1
    a, b = a_ref[...], b_ref[...]
    s_p = product(wi_ref.at[0], joined(jnp.where(even, a, b)))
    cat = joined(s_p)
    rest = jnp.where(even, b, a) - product(wq_ref, cat)
    s_q = product(wi_ref.at[1], joined(rest))
    part = product(wl_ref.at[0], cat) + product(wl_ref.at[1], joined(s_q))
    both_ways(even, -part, one_ref, two_ref)
    p_ref[...] = s_p
    q_ref[...] = s_q


def less_kernel(wl_ref, even_ref, p_ref, q_ref, acc_ref, one_ref, two_ref):
    part = product(wl_ref.at[0], joined(p_ref[...])) + product(wl_ref.at[1], joined(q_ref[...]))
    both_ways(even_ref[0] == 1, acc_ref[...] - part, one_ref, two_ref)


def merge_kernel(own_ref, x_ref, y_ref, mine_ref, out_ref):
    out_ref[...] = x_ref[...] + y_ref[...] + mine_ref[...] * own_ref[0].astype(F32)


def join_kernel(core_ref, own_ref, other_ref, out_ref):
    core = core_ref[0]
    n = own_ref.shape[0]
    for half, ref in ((core, own_ref), (1 - core, other_ref)):
        hi, lo = halves(ref[...])
        rows = pl.ds(pl.multiple_of(half * n, n), n)
        out_ref[0, rows, :] = hi
        out_ref[1, rows, :] = lo


def final_kernel(wi_ref, wq_ref, even_ref, a_ref, b_ref, c_ref, d_ref, *refs):
    known, out_ref = refs[:-1], refs[-1]
    even = even_ref[0] == 1
    one, two = a_ref[...] + c_ref[...], b_ref[...] + d_ref[...]
    s_p = product(wi_ref.at[0], joined(unpacked(jnp.where(even, one, two))))
    rest = unpacked(jnp.where(even, two, one)) - product(wq_ref, joined(s_p))
    s_q = product(wi_ref.at[1], joined(rest))
    n = s_p.shape[0] // 2
    for slot, s in ((0, s_p), (1, s_q)):
        old = functools.reduce(jnp.add, [k[...] for k in known[slot::2]])
        old = jnp.where(even, packed(old, 0), packed(old, 1))
        out_ref[slot] = old + jnp.concatenate([s[:n], s[n:]], axis=1)


def update_kernel(keep_ref, w0_ref, w1_ref, s_ref, out_ref, solved_ref):
    parts, _, rows, width = out_ref.shape
    steps, cuts = s_ref.shape[0] // 2, s_ref.shape[1]
    for slot in range(2):
        sides = []
        for half in range(cuts):
            pieces = [s_ref[slot * steps + j, half] for j in range(steps)]
            sides.append(unpacked(jnp.concatenate(pieces, axis=0)))
        solved_ref[slot] = jnp.concatenate(sides, axis=1)
    cats = [joined(solved_ref[slot]) for slot in range(2)]
    for a, w_ref in ((0, w0_ref), (1, w1_ref)):
        terms = [product(w_ref.at[slot], cats[slot]) for slot in range(2)]
        if a == 0:
            terms = [t * keep_ref[slot] for slot, t in enumerate(terms)]
        total = terms[0] + terms[1]
        for j in range(parts):
            out_ref[j, a] = total[j * rows : (j + 1) * rows]


def shards(panel, right_side, inverse_blocks):
    block = panel.shape[2]
    width = right_side.shape[3] // 2
    my_row, my_col = lax.axis_index("row"), lax.axis_index("col")
    row_count, col_count = lax.axis_size("row"), lax.axis_size("col")
    planes = row_count // 2
    plane, core = my_row // 2, my_row % 2
    core_arg = core.astype(jnp.int32).reshape(1)
    even = (1 - my_col % 2).astype(jnp.int32).reshape(1)
    whole = ((block, width), F32)
    slim = ((block // 2, width), F32)

    def send(array, moves):
        pairs = [
            ((2 * a + h) * col_count + b, (2 * c + h) * col_count + d)
            for (a, b), (c, d) in moves
            for h in range(2)
        ]
        return lax.ppermute(array, BOTH, pairs)

    def swap(array):
        return lax.ppermute(array, "row", [(r, r ^ 1) for r in range(row_count)])

    def flag(condition):
        return condition.astype(jnp.int32).reshape(1)

    inverse = inverse_blocks[0]
    rhs = lax.dynamic_slice(right_side, (0, 0, 0, core * width), (1, 1, block, width)).reshape(block, width)
    near = send(rhs, [((0, 0), (0, 1)), ((1, 0), (0, 2)), ((3, 0), (0, 3))])
    other_inverse = swap(inverse)
    tile = retile(after(panel, rhs), 0)
    other_tile = swap(tile)
    far = send(after(rhs, tile), [((z, 0), (0, 4 + z)) for z in range(4)])
    (wi,) = place(core_arg, inverse, other_inverse, 0)
    wl, ahead = place(core_arg, tile, after(other_tile, near), 1)

    firsts, thirds = [VMEM] * 2 + [SMEM] + [VMEM] * 3, [VMEM] * 5
    one = jnp.zeros((1,), jnp.int32)
    p_0, u = call(first_kernel, "first", 2, [whole] * 2, firsts, wi, wl, one, near, far, far)
    (s_q,) = call(second_kernel, "second", 1, [whole], [VMEM] * 3, wi, rhs, u)
    to_2 = send(s_q, [((0, 1), (0, 2))])
    to_3 = send(s_q, [((0, 1), (0, 3))])

    tile = retile(after(panel, s_q), 1)
    (wl1,) = place(core_arg, tile, swap(tile), 0)
    x = send(after(ahead, s_q), [((2, 5), (2, 6)), ((3, 7), (3, 6))])
    y = send(after(ahead, s_q), [((2, 5), (2, 7))])

    soon, q_0 = call(third_kernel, "third", 1, [whole] * 2, thirds, wl, rhs, u, after(to_2, wl1), to_3)
    a = send(soon, [((0, 2), (1, 3))])
    b = send(soon, [((0, 3), (1, 3)), ((0, 2), (1, 4))])
    c = send(soon, [((0, 2), (1, 5))])
    late_5 = send(after(s_q, soon), [((0, 1), (0, 5))])
    late_4 = send(after(s_q, soon), [((0, 1), (0, 4))])
    late_6 = send(q_0, [((0, 2), (0, 6)), ((0, 3), (0, 7))])
    later, _ = call(third_kernel, "later", 1, [whole] * 2, thirds + [VMEM], wl, rhs, u, late_4, late_5, late_6)
    acc = send(later, [((0, c), (1, c)) for c in range(4, 8)])

    own_flag = flag((plane == 3) & (my_col == 7))
    (got,) = call(
        merge_kernel, "merge", 0, [((block // 2, block), F32)], [SMEM] + [VMEM] * 3, own_flag, after(x, soon), y, ahead
    )
    wq = call(join_kernel, "join", 0, [((2, block, block), BF16)], [SMEM] + [VMEM] * 2, core_arg, got, swap(got))[0]

    a = after(a, wq)
    not_3 = flag(my_col != 3)
    p_1, u = call(first_kernel, "first", 2, [whole] * 2, firsts, wi, wl, not_3, a, b, c)
    (s_q,) = call(second_kernel, "second", 1, [whole], [VMEM] * 3, wi, b, u)
    to_4 = send(s_q, [((1, 3), (1, 4))])
    to_5 = send(s_q, [((1, 3), (1, 5))])

    soon, q_1 = call(third_kernel, "third", 1, [whole] * 2, thirds, wl, acc, u, to_4, to_5)
    a = send(soon, [((1, 4), (2, 6)), ((1, 5), (2, 7))])
    b = send(soon, [((1, 4), (2, 7)), ((1, 5), (2, 6))])
    late = [send(s, [((1, 4), (1, 6)), ((1, 5), (1, 7))]) for s in (p_1, q_1)]
    one, two = call(less_kernel, "less", 2, [slim] * 2, [VMEM, SMEM] + [VMEM] * 3, wl, even, *late, acc)
    c = send(one, [((1, 6), (3, 6)), ((1, 7), (3, 7))])
    d = send(two, [((1, 6), (3, 7)), ((1, 7), (3, 6))])

    specs = [VMEM] * 3 + [SMEM] + [VMEM] * 2
    one, two, p_2, q_2 = call(pair_kernel, "pair", 5, [slim] * 2 + [whole] * 2, specs, wi, wl, wq, even, a, b)
    a = send(one, [((2, 6), (3, 6)), ((2, 7), (3, 7))])
    b = send(two, [((2, 6), (3, 7)), ((2, 7), (3, 6))])

    specs = [VMEM] * 2 + [SMEM] + [VMEM] * 10
    known = (p_0, q_0, p_1, q_1, p_2, q_2)
    (mine,) = call(
        final_kernel, "final", 3, [((2, block // 2, width), F32)], specs, wi, wq, even, a, b, c, d, *known
    )

    cut = block // col_count
    pieces = lax.all_to_all(mine.reshape(col_count, cut, width), "col", 0, 0)
    root = jnp.array([2, 4, 6, 6])[plane]
    piece = lax.dynamic_slice_in_dim(pieces, root, 2, 0)
    pieces = lax.all_to_all(jnp.broadcast_to(piece[None], (col_count, 2, cut, width)), "col", 0, 0)

    keep = (my_col > 2 * plane + jnp.arange(2)).astype(F32)
    share = block // row_count
    outs = [((row_count, 2, share, width), F32), ((2, block, width), F32)]
    parts, mine = call(update_kernel, "update", 4, outs, [SMEM] + [VMEM] * 3, keep, wl, wl1, pieces)
    parts = lax.all_to_all(parts, "row", 0, 0)
    sums = parts.reshape(planes, 2, 2, share, width).sum(0)
    sums = jnp.concatenate([sums[0], sums[1]], axis=-1)
    own = lax.dynamic_slice_in_dim(right_side, my_row * share, share, 2).reshape(2, share, 2 * width)
    updated = (own - sums).reshape(2, 1, share, 2 * width)

    ours = jnp.where(core == 0, mine[0], mine[1])
    theirs = swap(jnp.where(core == 0, mine[1], mine[0]))
    solved = jnp.concatenate([jnp.where(core == 0, ours, theirs), jnp.where(core == 0, theirs, ours)], axis=1)
    return solved.reshape(1, block, 2 * width), updated


def solution(mesh):
    placed = (P(None, "col", None, "row", None), P(None, "col", None, None), P("row", None, None))
    return jax.shard_map(
        shards,
        mesh=mesh,
        in_specs=placed,
        out_specs=(P("row", None, None), P(None, "col", "row", None)),
        check_vma=False,
    )
```

time: 1330 us -> 300 us (0.23)
  waiting for transfers between devices: 1240 us -> 46.1 us
  starting transfers between devices: 0.65 us -> 132 us
  Pallas kernels: 0 us -> 62.3 us
  local copies, waits for them, and re-layouts: 25.8 us -> 51.8 us
  matrix products: 18.7 us -> 0 us
    psum x15 -> x0, waiting for transfers between devices: 1210 us -> none  [the longest x8 737 us: from_root(): return lax.psum(jnp.where(mine, array, jnp.zeros_like(array)), axis)]
    all_to_all x0 -> x3, starting transfers between devices: none -> 97.9 us  [the longest x1 60.9 us: shards(): parts = lax.all_to_all(parts, 'row', 0, 0)]
    pallas_call x0 -> x18, Pallas kernels: none -> 62.3 us  [the longest x13 44.6 us: call(): pl.pallas_call(kernel, out_shape=tuple((jax.ShapeDtypeStruct(shape, kind)...]
    unnamed x5 -> x62, local copies, waits for them, and re-layouts: 10.7 us -> 49 us
    all_to_all x0 -> x3, waiting for transfers between devices: none -> 36.4 us  [the longest x1 14.7 us: shards(): lax.all_to_all(jnp.broadcast_to(piece[None], (col_count, 2, cut, width)),...]
    reduce_scatter x1 -> x0, waiting for transfers between devices: 35.3 us -> none  [shards(): lax.psum_scatter(partial_value, 'row', scatter_dimension=1, tiled=True)]
    ppermute x0 -> x28, starting transfers between devices: none -> 34.5 us  [the longest x23 27.7 us: send(): return lax.ppermute(array, BOTH, pairs)]
    dot_general x2 -> x0, matrix products: 18.7 us -> none  [the longest x1 9.39 us: shards(): jnp.dot(inverse, rhs_local[0] - total, precision=highest)]
  transfers between devices with their start and end apart: 16 -> 31, of which waited for: 16 -> 5; matrix products, arithmetic and copies ran while one was open for 1% -> 1% of each run, Pallas kernels for 0% -> 11%
where the time goes in v2:
time: 300 us; the launch traced here: 299 us
  starting transfers between devices  132 us (44%)
  Pallas kernels  62.3 us (21%)
  local copies, waits for them, and re-layouts  51.8 us (17%)
  waiting for transfers between devices  46.1 us (15%)
  between operations  3.14 us (1%)
    all_to_all x1, starting transfers between devices, shards(): parts = lax.all_to_all(parts, 'row', 0, 0)  60.9 us
    unnamed x62, local copies, waits for them, and re-layouts  49 us
    pallas_call x13, Pallas kernels, call(): pl.pallas_call(kernel, out_shape=tuple((jax.ShapeDtypeStruct(shape, kind)...  44.6 us
    all_to_all x1, starting transfers between devices, shards(): pieces = lax.all_to_all(mine.reshape(col_count, cut, width), 'col', 0, 0)  33.3 us
    ppermute x23, starting transfers between devices, send(): return lax.ppermute(array, BOTH, pairs)  27.7 us
    all_to_all x1, waiting for transfers between devices, shards(): lax.all_to_all(jnp.broadcast_to(piece[None], (col_count, 2, cut, width)),...  14.7 us
    all_to_all x1, waiting for transfers between devices, shards(): parts = lax.all_to_all(parts, 'row', 0, 0)  14 us
    ppermute x23, waiting for transfers between devices, send(): return lax.ppermute(array, BOTH, pairs)  9.57 us
  transfers between devices with their start and end apart: 31, of which 5 were waited for; matrix products, arithmetic and copies ran while one was open for 1% of the time, Pallas kernels for 11%

profile of v2, /device:TPU:1, one launch (start us, length us, event | category | flops | bytes accessed | tf_op | source)
XLA Modules:
  0.0 298.7 jit_solution(4459020412552622718)
XLA Ops:
  1.7 4.3 %retile.2.own_ref = f32[1024,1024]{1,0:T(8,128)} custom-call(f32[2,1,1024,1,1024]{4,3,2,1,0:T(1,128)} %panel_ref.1), custom_call_target="tpu_custom_call" | custom-call | flops 1 | bytes 1 | tf_op jit(solution)/shard_map/retile/pallas_call | solution.py:75
  7.7 3.3 %collective-permute-start.1 = (f32[1024,128]{1,0:T(8,128)S(1)}, f32[1024,128]{1,0:T(8,128)S(1)}, u32[]{:S(2)}, u32[]{:S(2)}) collective-permute-start(f32[1024,128]{1,0:T(8,128)S(1)} %dynamic-slice_bitcast_fusion.r_ref.acc_ref), channel_id=1, source_target_pairs={{0,1},{16,17},{32,2},{48,18},{96,3},{112,19}} | collective-permute-start | bytes 1572872 | tf_op jit(solution)/shard_map/ppermute | solution.py:230
  12.3 9.5 %collective-permute-done.1.a_ref = f32[1024,128]{1,0:T(8,128)S(1)} collective-permute-done((f32[1024,128]{1,0:T(8,128)S(1)}, f32[1024,128]{1,0:T(8,128)S(1)}, u32[]{:S(2)}, u32[]{:S(2)}) %collective-permute-start.1) | collective-permute-done | bytes 524320 | tf_op jit(solution)/shard_map/ppermute | solution.py:230
  27.8 5.0 %copy-done = bf16[2,2,1024,1024]{3,2,1,0:T(8,128)(2,1)} copy-done((bf16[2,2,1024,1024]{3,2,1,0:T(8,128)(2,1)}, bf16[2,2,1024,1024]{3,2,1,0:T(8,128)(2,1)S(1)}, u32[]{:S(2)}) %copy-start) | copy-done | bytes 8388632
  37.2 4.9 %retile.3.own_ref = f32[1024,1024]{1,0:T(8,128)} custom-call(f32[2,1,1024,1,1024]{4,3,2,1,0:T(1,128)S(1)} %bitcast.26), custom_call_target="tpu_custom_call" | custom-call | flops 1 | bytes 1 | tf_op jit(solution)/shard_map/retile/pallas_call | solution.py:75
  50.6 4.9 %place.5.w1_ref = bf16[2,2,1024,1024]{3,2,1,0:T(8,128)(2,1)S(1)} custom-call(s32[1]{0:T(128)} %bitcast.core_ref, f32[1024,1024]{1,0:T(8,128)} %retile.3.own_ref, f32[1024,1024]{1,0:T(8,128)} %collective-permute-done.4.other_ref), custom_call_target="tpu_custom_call" | custom-call | flops 1 | bytes 1 | tf_op jit(solution)/shard_map/place/pallas_call | solution.py:108
  55.5 3.3 %copy-done.14 = bf16[2,2,1024,1024]{3,2,1,0:T(8,128)(2,1)} copy-done((bf16[2,2,1024,1024]{3,2,1,0:T(8,128)(2,1)}, bf16[2,2,1024,1024]{3,2,1,0:T(8,128)(2,1)S(1)}, u32[]{:S(2)}) %copy-start.14) | copy-done | bytes 8388632
  58.8 3.4 %copy-done.1 = bf16[2,2,1024,1024]{3,2,1,0:T(8,128)(2,1)S(1)} copy-done((bf16[2,2,1024,1024]{3,2,1,0:T(8,128)(2,1)S(1)}, bf16[2,2,1024,1024]{3,2,1,0:T(8,128)(2,1)}, u32[]{:S(2)}) %copy-start.1) | copy-done | bytes 8388632
  62.2 3.3 %third.2 = (f32[1024,128]{1,0:T(8,128)}, f32[1024,128]{1,0:T(8,128)}) custom-call(bf16[2,2,1024,1024]{3,2,1,0:T(8,128)(2,1)S(1)} %copy-done.1, f32[1024,128]{1,0:T(8,128)S(1)} %dynamic-slice_bitcast_fusion.r_ref.acc_ref, f32[1024,128]{1,0:T(8,128)S(1)} %get-tuple-element.34.u_ref, f32[1024,128]{1,0:T(8,128)} %collective-permute-done.6.refs_0_, ...), custom_call_target="tpu_custom_call" | custom-call | flops 1 | bytes 1 | tf_op jit(solution)/shard_map/third/pallas_call | solution.py:52
  65.5 2.5 merge.1.own_ref
  77.3 3.4 %copy-done.2 = bf16[2,2,1024,1024]{3,2,1,0:T(8,128)(2,1)S(1)} copy-done((bf16[2,2,1024,1024]{3,2,1,0:T(8,128)(2,1)S(1)}, bf16[2,2,1024,1024]{3,2,1,0:T(8,128)(2,1)}, u32[]{:S(2)}) %copy-start.2) | copy-done | bytes 8388632
  82.8 2.6 later.1
  90.8 3.4 %copy-done.3 = bf16[2,2,1024,1024]{3,2,1,0:T(8,128)(2,1)S(1)} copy-done((bf16[2,2,1024,1024]{3,2,1,0:T(8,128)(2,1)S(1)}, bf16[2,2,1024,1024]{3,2,1,0:T(8,128)(2,1)}, u32[]{:S(2)}) %copy-start.3) | copy-done | bytes 8388632
  94.1 3.4 %copy-done.7 = bf16[2,2,1024,1024]{3,2,1,0:T(8,128)(2,1)S(1)} copy-done((bf16[2,2,1024,1024]{3,2,1,0:T(8,128)(2,1)S(1)}, bf16[2,2,1024,1024]{3,2,1,0:T(8,128)(2,1)}, u32[]{:S(2)}) %copy-start.7) | copy-done | bytes 8388632
  97.5 3.9 %first.3 = (f32[1024,128]{1,0:T(8,128)S(1)}, f32[1024,128]{1,0:T(8,128)S(1)}) custom-call(bf16[2,2,1024,1024]{3,2,1,0:T(8,128)(2,1)S(1)} %copy-done.7, bf16[2,2,1024,1024]{3,2,1,0:T(8,128)(2,1)S(1)} %copy-done.3, s32[1]{0:T(128)} %bitcast.5.flag_ref, f32[1024,128]{1,0:T(8,128)} %collective-permute-done.14.a_ref, ...), custom_call_target="tpu_custom_call" | custom-call | flops 1 | bytes 1 | tf_op jit(solution)/shard_map/first/pallas_call | solution.py:52
  101.4 2.5 second.3
  111.1 3.4 %copy-done.4 = bf16[2,2,1024,1024]{3,2,1,0:T(8,128)(2,1)S(1)} copy-done((bf16[2,2,1024,1024]{3,2,1,0:T(8,128)(2,1)S(1)}, bf16[2,2,1024,1024]{3,2,1,0:T(8,128)(2,1)}, u32[]{:S(2)}) %copy-start.4) | copy-done | bytes 8388632
  114.4 3.4 %copy-done.9 = bf16[2,2,1024,1024]{3,2,1,0:T(8,128)(2,1)S(1)} copy-done((bf16[2,2,1024,1024]{3,2,1,0:T(8,128)(2,1)S(1)}, bf16[2,2,1024,1024]{3,2,1,0:T(8,128)(2,1)}, u32[]{:S(2)}) %copy-start.9) | copy-done | bytes 8388632
  120.0 6.7 %pair.1 = (f32[512,128]{1,0:T(8,128)S(1)}, f32[512,128]{1,0:T(8,128)S(1)}, f32[1024,128]{1,0:T(8,128)S(1)}, f32[1024,128]{1,0:T(8,128)S(1)}) custom-call(bf16[2,2,1024,1024]{3,2,1,0:T(8,128)(2,1)S(1)} %copy-done.9, bf16[2,2,1024,1024]{3,2,1,0:T(8,128)(2,1)S(1)} %copy-done.4, bf16[2,1024,1024]{2,1,0:T(8,128)(2,1)S(1)} %copy-done.12, s32[1]{0:T(128)} %bitcast.4.even_ref, ...), custom_call_target="tpu_custom_call" | custom-call | flops 1 | bytes 1 | tf_op jit(solution)/shard_map/pair/pallas_call | solution.py:52
  128.5 2.4 less.1
  132.4 3.4 %copy-done.10 = bf16[2,2,1024,1024]{3,2,1,0:T(8,128)(2,1)S(1)} copy-done((bf16[2,2,1024,1024]{3,2,1,0:T(8,128)(2,1)S(1)}, bf16[2,2,1024,1024]{3,2,1,0:T(8,128)(2,1)}, u32[]{:S(2)}) %copy-start.10) | copy-done | bytes 8388632
  135.7 5.7 %final.1 = f32[2,512,128]{2,1,0:T(8,128)} custom-call(bf16[2,2,1024,1024]{3,2,1,0:T(8,128)(2,1)S(1)} %copy-done.10, bf16[2,1024,1024]{2,1,0:T(8,128)(2,1)S(1)} %copy-done.13, s32[1]{0:T(128)} %bitcast.4.even_ref, f32[512,128]{1,0:T(8,128)S(1)} %collective-permute-done.21.a_ref, f32[512,128]{1,0:T(8,128)S(1)} %collective-permute-done.22.b_ref, ...), custom_call_target="tpu_custom_call" | custom-call | flops 1 | bytes 1 | tf_op jit(solution)/shard_map/final/pallas_call | solution.py:52
  141.4 33.3 %all-to-all-start = ((f32[16,64,128]{2,1,0:T(8,128)}), f32[16,64,128]{2,1,0:T(8,128)S(1)}, u32[]{:S(2)}, u32[]{:S(2)}) async-start(f32[16,64,128]{2,1,0:T(8,128)} %bitcast.6), calls=%async_computation | async-start | bytes 1048576 | tf_op jit(solution)/shard_map/all_to_all | solution.py:303
  177.2 7.8 %all-to-all-done = f32[16,64,128]{2,1,0:T(8,128)S(1)} async-done(((f32[16,64,128]{2,1,0:T(8,128)}), f32[16,64,128]{2,1,0:T(8,128)S(1)}, u32[]{:S(2)}, u32[]{:S(2)}) %all-to-all-start) | async-done | bytes 524320 | tf_op jit(solution)/shard_map/all_to_all | solution.py:303
  186.1 3.7 %all-to-all-start.1 = ((f32[16,2,64,128]{3,2,1,0:T(8,128)}), f32[16,2,64,128]{3,2,1,0:T(8,128)S(1)}, u32[]{:S(2)}, u32[]{:S(2)}) async-start(f32[16,2,64,128]{3,2,1,0:T(8,128)} %broadcast_in_dim.2), calls=%async_computation.1 | async-start | bytes 2097152 | tf_op jit(solution)/shard_map/all_to_all | solution.py:306
  189.8 14.7 %all-to-all-done.1.s_ref = f32[16,2,64,128]{3,2,1,0:T(8,128)S(1)} async-done(((f32[16,2,64,128]{3,2,1,0:T(8,128)}), f32[16,2,64,128]{3,2,1,0:T(8,128)S(1)}, u32[]{:S(2)}, u32[]{:S(2)}) %all-to-all-start.1) | async-done | bytes 1048608 | tf_op jit(solution)/shard_map/all_to_all | solution.py:306
  204.5 3.4 %copy-done.5 = bf16[2,2,1024,1024]{3,2,1,0:T(8,128)(2,1)S(1)} copy-done((bf16[2,2,1024,1024]{3,2,1,0:T(8,128)(2,1)S(1)}, bf16[2,2,1024,1024]{3,2,1,0:T(8,128)(2,1)}, u32[]{:S(2)}) %copy-start.5) | copy-done | bytes 8388632
  207.9 3.4 %copy-done.15 = bf16[2,2,1024,1024]{3,2,1,0:T(8,128)(2,1)S(1)} copy-done((bf16[2,2,1024,1024]{3,2,1,0:T(8,128)(2,1)S(1)}, bf16[2,2,1024,1024]{3,2,1,0:T(8,128)(2,1)}, u32[]{:S(2)}) %copy-start.15) | copy-done | bytes 8388632
  211.3 6.1 %update.1 = (f32[8,2,128,128]{3,2,1,0:T(8,128)}, f32[2,1024,128]{2,1,0:T(8,128)S(1)}) custom-call(f32[2]{0:T(128)S(1)} %compare_convert_fusion.keep_ref, bf16[2,2,1024,1024]{3,2,1,0:T(8,128)(2,1)S(1)} %copy-done.5, bf16[2,2,1024,1024]{3,2,1,0:T(8,128)(2,1)S(1)} %copy-done.15, f32[16,2,64,128]{3,2,1,0:T(8,128)S(1)} %all-to-all-done.1.s_ref), custom_call_target="tpu_custom_call" | custom-call | flops 1 | bytes 1 | tf_op jit(solution)/shard_map/update/pallas_call | solution.py:52
  217.5 3.4 %collective-permute-start.27 = (f32[1024,128]{1,0:T(8,128)S(1)}, f32[1024,128]{1,0:T(8,128)S(1)}, u32[]{:S(2)}, u32[]{:S(2)}) collective-permute-start(f32[1024,128]{1,0:T(8,128)S(1)} %select_bitcast_fusion), channel_id=1, source_target_pairs={{0,16},{16,0},{32,48},{48,32},{64,80},{80,64},{96,112},{112,96},{1... | collective-permute-start | bytes 1572872 | tf_op jit(solution)/shard_map/ppermute | solution.py:233
  220.8 60.9 %all-to-all-start.2 = ((f32[8,2,128,128]{3,2,1,0:T(8,128)}), f32[8,2,128,128]{3,2,1,0:T(8,128)S(1)}, u32[]{:S(2)}, u32[]{:S(2)}) async-start(f32[8,2,128,128]{3,2,1,0:T(8,128)} %get-tuple-element.57), calls=%async_computation.2 | async-start | bytes 2097152 | tf_op jit(solution)/shard_map/all_to_all | solution.py:312
  282.9 14.0 %all-to-all-done.2 = f32[8,2,128,128]{3,2,1,0:T(8,128)S(1)} async-done(((f32[8,2,128,128]{3,2,1,0:T(8,128)}), f32[8,2,128,128]{3,2,1,0:T(8,128)S(1)}, u32[]{:S(2)}, u32[]{:S(2)}) %all-to-all-start.2) | async-done | bytes 1048608 | tf_op jit(solution)/shard_map/all_to_all | solution.py:312
  (123 shorter events, 56.4 us)
Async XLA Ops:
  6.1 15.8 %collective-permute-start = (f32[1024,1024]{1,0:T(8,128)}, f32[1024,1024]{1,0:T(8,128)S(1)}, u32[]{:S(2)}, u32[]{:S(2)}) collective-permute-start(f32[1024,1024]{1,0:T(8,128)} %retile.2.own_ref), channel_id=1, source_target_pairs={{0,16},{16,0},{32,48},{48,32},{64,80},{80,64},{96,112},{112,96},{1... | collective-permute-start | bytes 12582920 | tf_op jit(solution)/shard_map/ppermute | solution.py:233
  7.6 18.4 %collective-permute-start.2 = (f32[1024,1024]{1,0:T(8,128)S(1)}, f32[1024,1024]{1,0:T(8,128)S(1)}, u32[]{:S(2)}, u32[]{:S(2)}) collective-permute-start(f32[1024,1024]{1,0:T(8,128)S(1)} %bitcast.27), channel_id=1, source_target_pairs={{0,16},{16,0},{32,48},{48,32},{64,80},{80,64},{96,112},{112,96},{1... | collective-permute-start | bytes 12582920 | tf_op jit(solution)/shard_map/ppermute | solution.py:233
  7.7 14.2 %collective-permute-start.1 = (f32[1024,128]{1,0:T(8,128)S(1)}, f32[1024,128]{1,0:T(8,128)S(1)}, u32[]{:S(2)}, u32[]{:S(2)}) collective-permute-start(f32[1024,128]{1,0:T(8,128)S(1)} %dynamic-slice_bitcast_fusion.r_ref.acc_ref), channel_id=1, source_target_pairs={{0,1},{16,17},{32,2},{48,18},{96,3},{112,19}} | collective-permute-start | bytes 1572872 | tf_op jit(solution)/shard_map/ppermute | solution.py:230
  11.0 16.7 %collective-permute-start.3 = (f32[1024,128]{1,0:T(8,128)S(1)}, f32[1024,128]{1,0:T(8,128)S(1)}, u32[]{:S(2)}, u32[]{:S(2)}) collective-permute-start(f32[1024,128]{1,0:T(8,128)S(1)} %dynamic-slice_bitcast_fusion.r_ref.acc_ref), channel_id=1, source_target_pairs={{0,4},{16,20},{32,5},{48,21},{64,6},{80,22},{96,7},{112,23}} | collective-permute-start | bytes 1572872 | tf_op jit(solution)/shard_map/ppermute | solution.py:230
  42.1 8.5 %collective-permute-start.4 = (f32[1024,1024]{1,0:T(8,128)}, f32[1024,1024]{1,0:T(8,128)}, u32[]{:S(2)}, u32[]{:S(2)}) collective-permute-start(f32[1024,1024]{1,0:T(8,128)} %retile.3.own_ref), channel_id=1, source_target_pairs={{0,16},{16,0},{32,48},{48,32},{64,80},{80,64},{96,112},{112,96},{1... | collective-permute-start | bytes 12582920 | tf_op jit(solution)/shard_map/ppermute | solution.py:233
  43.5 22.0 %collective-permute-start.5 = (f32[512,1024]{1,0:T(8,128)S(1)}, f32[512,1024]{1,0:T(8,128)}, u32[]{:S(2)}, u32[]{:S(2)}) collective-permute-start(f32[512,1024]{1,0:T(8,128)S(1)} %get-tuple-element.37.mine_ref), channel_id=1, source_target_pairs={{69,70},{85,86},{103,102},{119,118}} | collective-permute-start | bytes 6291464 | tf_op jit(solution)/shard_map/ppermute | solution.py:230
  45.6 19.9 %collective-permute-start.8 = (f32[512,1024]{1,0:T(8,128)S(1)}, f32[512,1024]{1,0:T(8,128)}, u32[]{:S(2)}, u32[]{:S(2)}) collective-permute-start(f32[512,1024]{1,0:T(8,128)S(1)} %get-tuple-element.37.mine_ref), channel_id=1, source_target_pairs={{69,71},{85,87}} | collective-permute-start | bytes 6291464 | tf_op jit(solution)/shard_map/ppermute | solution.py:230
  47.5 11.3 %collective-permute-start.6 = (f32[1024,128]{1,0:T(8,128)}, f32[1024,128]{1,0:T(8,128)}, u32[]{:S(2)}, u32[]{:S(2)}) collective-permute-start(f32[1024,128]{1,0:T(8,128)} %second.2), channel_id=1, source_target_pairs={{1,2},{17,18}} | collective-permute-start | bytes 1572872 | tf_op jit(solution)/shard_map/ppermute | solution.py:230
  49.0 9.8 %collective-permute-start.7 = (f32[1024,128]{1,0:T(8,128)}, f32[1024,128]{1,0:T(8,128)}, u32[]{:S(2)}, u32[]{:S(2)}) collective-permute-start(f32[1024,128]{1,0:T(8,128)} %second.2), channel_id=1, source_target_pairs={{1,3},{17,19}} | collective-permute-start | bytes 1572872 | tf_op jit(solution)/shard_map/ppermute | solution.py:230
  68.0 18.3 %collective-permute-start.9 = (f32[512,1024]{1,0:T(8,128)S(1)}, f32[512,1024]{1,0:T(8,128)}, u32[]{:S(2)}, u32[]{:S(2)}) collective-permute-start(f32[512,1024]{1,0:T(8,128)S(1)} %merge.1.own_ref), channel_id=1, source_target_pairs={{0,16},{16,0},{32,48},{48,32},{64,80},{80,64},{96,112},{112,96},{1... | collective-permute-start | bytes 6291464 | tf_op jit(solution)/shard_map/ppermute | solution.py:233
  68.5 4.3 %collective-permute-start.10 = (f32[1024,128]{1,0:T(8,128)}, f32[1024,128]{1,0:T(8,128)S(1)}, u32[]{:S(2)}, u32[]{:S(2)}) collective-permute-start(f32[1024,128]{1,0:T(8,128)} %second.2), channel_id=1, source_target_pairs={{1,4},{17,20}} | collective-permute-start | bytes 1572872 | tf_op jit(solution)/shard_map/ppermute | solution.py:230
  69.2 5.9 %collective-permute-start.11 = (f32[1024,128]{1,0:T(8,128)}, f32[1024,128]{1,0:T(8,128)S(1)}, u32[]{:S(2)}, u32[]{:S(2)}) collective-permute-start(f32[1024,128]{1,0:T(8,128)} %second.2), channel_id=1, source_target_pairs={{1,5},{17,21}} | collective-permute-start | bytes 1572872 | tf_op jit(solution)/shard_map/ppermute | solution.py:230
  69.9 7.5 %collective-permute-start.12 = (f32[1024,128]{1,0:T(8,128)}, f32[1024,128]{1,0:T(8,128)}, u32[]{:S(2)}, u32[]{:S(2)}) collective-permute-start(f32[1024,128]{1,0:T(8,128)} %get-tuple-element.42.refs_1_), channel_id=1, source_target_pairs={{2,6},{18,22},{3,7},{19,23}} | collective-permute-start | bytes 1572872 | tf_op jit(solution)/shard_map/ppermute | solution.py:230
  71.3 19.4 %collective-permute-start.14 = (f32[1024,128]{1,0:T(8,128)}, f32[1024,128]{1,0:T(8,128)}, u32[]{:S(2)}, u32[]{:S(2)}) collective-permute-start(f32[1024,128]{1,0:T(8,128)} %get-tuple-element.39), channel_id=1, source_target_pairs={{2,35},{18,51}} | collective-permute-start | bytes 1572872 | tf_op jit(solution)/shard_map/ppermute | solution.py:230
  73.6 17.1 %collective-permute-start.15 = (f32[1024,128]{1,0:T(8,128)}, f32[1024,128]{1,0:T(8,128)}, u32[]{:S(2)}, u32[]{:S(2)}) collective-permute-start(f32[1024,128]{1,0:T(8,128)} %get-tuple-element.39), channel_id=1, source_target_pairs={{3,35},{19,51},{2,36},{18,52}} | collective-permute-start | bytes 1572872 | tf_op jit(solution)/shard_map/ppermute | solution.py:230
  75.9 14.9 %collective-permute-start.16 = (f32[1024,128]{1,0:T(8,128)}, f32[1024,128]{1,0:T(8,128)}, u32[]{:S(2)}, u32[]{:S(2)}) collective-permute-start(f32[1024,128]{1,0:T(8,128)} %get-tuple-element.39), channel_id=1, source_target_pairs={{2,37},{18,53}} | collective-permute-start | bytes 1572872 | tf_op jit(solution)/shard_map/ppermute | solution.py:230
  85.4 19.9 %collective-permute-start.13 = (f32[1024,128]{1,0:T(8,128)S(1)}, f32[1024,128]{1,0:T(8,128)S(1)}, u32[]{:S(2)}, u32[]{:S(2)}) collective-permute-start(f32[1024,128]{1,0:T(8,128)S(1)} %get-tuple-element.43), channel_id=1, source_target_pairs={{4,36},{20,52},{5,37},{21,53},{6,38},{22,54},{7,39},{23,55}} | collective-permute-start | bytes 1572872 | tf_op jit(solution)/shard_map/ppermute | solution.py:230
  103.9 1.4 collective-permute-start.17
  104.6 0.7 collective-permute-start.18
  107.5 3.6 %collective-permute-start.19 = (f32[1024,128]{1,0:T(8,128)}, f32[1024,128]{1,0:T(8,128)S(1)}, u32[]{:S(2)}, u32[]{:S(2)}) collective-permute-start(f32[1024,128]{1,0:T(8,128)} %get-tuple-element.46), channel_id=1, source_target_pairs={{36,70},{52,86},{37,71},{53,87}} | collective-permute-start | bytes 1572872 | tf_op jit(solution)/shard_map/ppermute | solution.py:230
  108.1 2.9 collective-permute-start.20
  109.6 18.9 %collective-permute-start.23 = (f32[1024,128]{1,0:T(8,128)S(1)}, f32[1024,128]{1,0:T(8,128)S(1)}, u32[]{:S(2)}, u32[]{:S(2)}) collective-permute-start(f32[1024,128]{1,0:T(8,128)S(1)} %get-tuple-element.49.refs_2_), channel_id=1, source_target_pairs={{36,38},{52,54},{37,39},{53,55}} | collective-permute-start | bytes 1572872 | tf_op jit(solution)/shard_map/ppermute | solution.py:230
  110.3 18.2 %collective-permute-start.24 = (f32[1024,128]{1,0:T(8,128)S(1)}, f32[1024,128]{1,0:T(8,128)S(1)}, u32[]{:S(2)}, u32[]{:S(2)}) collective-permute-start(f32[1024,128]{1,0:T(8,128)S(1)} %get-tuple-element.50.refs_3_), channel_id=1, source_target_pairs={{36,38},{52,54},{37,39},{53,55}} | collective-permute-start | bytes 1572872 | tf_op jit(solution)/shard_map/ppermute | solution.py:230
  126.7 5.6 %collective-permute-start.21 = (f32[512,128]{1,0:T(8,128)S(1)}, f32[512,128]{1,0:T(8,128)S(1)}, u32[]{:S(2)}, u32[]{:S(2)}) collective-permute-start(f32[512,128]{1,0:T(8,128)S(1)} %get-tuple-element.47), channel_id=1, source_target_pairs={{70,102},{86,118},{71,103},{87,119}} | collective-permute-start | bytes 786440 | tf_op jit(solution)/shard_map/ppermute | solution.py:230
  127.4 4.9 %collective-permute-start.22 = (f32[512,128]{1,0:T(8,128)S(1)}, f32[512,128]{1,0:T(8,128)S(1)}, u32[]{:S(2)}, u32[]{:S(2)}) collective-permute-start(f32[512,128]{1,0:T(8,128)S(1)} %get-tuple-element.48), channel_id=1, source_target_pairs={{70,103},{86,119},{71,102},{87,118}} | collective-permute-start | bytes 786440 | tf_op jit(solution)/shard_map/ppermute | solution.py:230
  130.9 1.4 collective-permute-start.25
  131.6 0.7 collective-permute-start.26
  135.7 39.0 %copy-start.26 = (s32[4]{0:T(128)S(1)}, s32[4]{0:T(128)}, u32[]{:S(2)}) copy-start(s32[4]{0:T(128)} %constant.59.clone) | copy-start | bytes 52
  141.4 43.6 %all-to-all-start = ((f32[16,64,128]{2,1,0:T(8,128)}), f32[16,64,128]{2,1,0:T(8,128)S(1)}, u32[]{:S(2)}, u32[]{:S(2)}) async-start(f32[16,64,128]{2,1,0:T(8,128)} %bitcast.6), calls=%async_computation | async-start | bytes 1048576 | tf_op jit(solution)/shard_map/all_to_all | solution.py:303
  186.1 18.4 %all-to-all-start.1 = ((f32[16,2,64,128]{3,2,1,0:T(8,128)}), f32[16,2,64,128]{3,2,1,0:T(8,128)S(1)}, u32[]{:S(2)}, u32[]{:S(2)}) async-start(f32[16,2,64,128]{3,2,1,0:T(8,128)} %broadcast_in_dim.2), calls=%async_computation.1 | async-start | bytes 2097152 | tf_op jit(solution)/shard_map/all_to_all | solution.py:306
  217.5 64.3 %collective-permute-start.27 = (f32[1024,128]{1,0:T(8,128)S(1)}, f32[1024,128]{1,0:T(8,128)S(1)}, u32[]{:S(2)}, u32[]{:S(2)}) collective-permute-start(f32[1024,128]{1,0:T(8,128)S(1)} %select_bitcast_fusion), channel_id=1, source_target_pairs={{0,16},{16,0},{32,48},{48,32},{64,80},{80,64},{96,112},{112,96},{1... | collective-permute-start | bytes 1572872 | tf_op jit(solution)/shard_map/ppermute | solution.py:233
  220.8 76.0 %all-to-all-start.2 = ((f32[8,2,128,128]{3,2,1,0:T(8,128)}), f32[8,2,128,128]{3,2,1,0:T(8,128)S(1)}, u32[]{:S(2)}, u32[]{:S(2)}) async-start(f32[8,2,128,128]{3,2,1,0:T(8,128)} %get-tuple-element.57), calls=%async_computation.2 | async-start | bytes 2097152 | tf_op jit(solution)/shard_map/all_to_all | solution.py:312
  (30 other events, 157.0 us)

commit v3 on v2

v3 whole, which is shorter than its diff:
```python
import functools

import jax
import jax.numpy as jnp
from jax import lax
from jax.experimental import pallas as pl
from jax.experimental.pallas import tpu as pltpu
from jax.sharding import PartitionSpec as P

F32 = jnp.float32
BF16 = jnp.bfloat16
LIMIT = 12 * 1024 * 1024
BOTH = ("row", "col")
VMEM = pl.BlockSpec(memory_space=pltpu.VMEM)
SMEM = pl.BlockSpec(memory_space=pltpu.SMEM)
ANY = pl.BlockSpec(memory_space=pl.ANY)


def halves(x):
    hi = x.astype(BF16)
    return hi, (x - hi.astype(F32)).astype(BF16)


def joined(x):
    return jnp.concatenate(halves(x), axis=1)


def product(w, cat):
    width = cat.shape[1] // 2
    hi, lo = halves(w)
    one = jnp.dot(hi, cat, preferred_element_type=F32)
    two = jnp.dot(lo, cat[:, :width], preferred_element_type=F32)
    return one[:, :width] + one[:, width:] + two


class Pair:
    def __init__(self, core_ref, own_ref, other_ref):
        self.first, self.refs = core_ref[0] == 0, (own_ref, other_ref)

    def __getitem__(self, slot):
        own, other = (ref[...] for ref in self.refs)
        return jnp.where(self.first, own, other) if slot == 0 else jnp.where(self.first, other, own)


def stacked(core_ref, own_ref, other_ref, cat):
    first = core_ref[0] == 0
    own, other = product(own_ref[...], cat), product(other_ref[...], cat)
    return jnp.concatenate([jnp.where(first, own, other), jnp.where(first, other, own)], axis=0)


def packed(x, half):
    n, width = x.shape
    part = x[:, half * width // 2 : (half + 1) * width // 2]
    return jnp.concatenate([part[: n // 2], part[n // 2 :]], axis=1)


def unpacked(x):
    width = x.shape[1] // 2
    return jnp.concatenate([x[:, :width], x[:, width:]], axis=0)


def cost(flops, nbytes):
    return pl.CostEstimate(flops=flops, bytes_accessed=nbytes, transcendentals=0)


def call(kernel, name, products, outs, specs, *args):
    n = 1024
    return pl.pallas_call(
        kernel,
        out_shape=tuple(jax.ShapeDtypeStruct(shape, kind) for shape, kind in outs),
        in_specs=specs,
        out_specs=(VMEM,) * len(outs),
        compiler_params=pltpu.CompilerParams(vmem_limit_bytes=LIMIT),
        cost_estimate=cost(6 * products * n * n * 128, 4 * products * n * n),
        name=name,
    )(*args)


def after(x, *others):
    return lax.optimization_barrier((x,) + others)[0]


def retile_kernel(a, panel_ref, out_ref, sem):
    copy = pltpu.make_async_copy(panel_ref.at[a, 0, :, 0], out_ref, sem.at[0])
    copy.start()
    copy.wait()


def retile(panel, a):
    n, depth = panel.shape[2], panel.shape[4]
    return pl.pallas_call(
        functools.partial(retile_kernel, a),
        out_shape=jax.ShapeDtypeStruct((n, depth), F32),
        in_specs=[pl.BlockSpec(memory_space=pltpu.HBM)],
        out_specs=VMEM,
        scratch_shapes=[pltpu.SemaphoreType.DMA((1,))],
        compiler_params=pltpu.CompilerParams(vmem_limit_bytes=(56 - 40 * a) * 1024 * 1024),
        cost_estimate=cost(0, 8 * n * depth),
        name="retile",
    )(panel)


def cut_kernel(core_ref, own_ref, other_ref, out_ref):
    n = out_ref.shape[0]

    @pl.when(core_ref[0] == 0)
    def _():
        out_ref[...] = own_ref[:n]

    @pl.when(core_ref[0] == 1)
    def _():
        out_ref[...] = other_ref[n:]


def first_kernel(core_ref, flag_ref, io_ref, ix_ref, lo_ref, lx_ref, a_ref, b_ref, c_ref, s_ref, u_ref):
    r = a_ref[...] + c_ref[...] + b_ref[...] * flag_ref[0].astype(F32)
    s = product(Pair(core_ref, io_ref, ix_ref)[0], joined(r))
    s_ref[...] = s
    u_ref[...] = product(Pair(core_ref, lo_ref, lx_ref)[0], joined(s))


def second_kernel(core_ref, io_ref, ix_ref, r_ref, u_ref, s_ref):
    s_ref[...] = product(Pair(core_ref, io_ref, ix_ref)[1], joined(r_ref[...] - u_ref[...]))


def third_kernel(core_ref, lo_ref, lx_ref, acc_ref, u_ref, *refs):
    parts, out_ref, sum_ref = refs[:-2], refs[-2], refs[-1]
    s = functools.reduce(jnp.add, [p[...] for p in parts])
    sum_ref[...] = s
    out_ref[...] = acc_ref[...] - u_ref[...] - product(Pair(core_ref, lo_ref, lx_ref)[1], joined(s))


def both_ways(even, x, one_ref, two_ref):
    low, high = packed(x, 0), packed(x, 1)
    one_ref[...] = jnp.where(even, low, high)
    two_ref[...] = jnp.where(even, high, low)


def pair_kernel(
    core_ref, even_ref, io_ref, ix_ref, lo_ref, lx_ref, qo_ref, qx_ref, a_ref, b_ref, one_ref, two_ref, p_ref, q_ref
):
    even = even_ref[0] == 1
    inverse, below = Pair(core_ref, io_ref, ix_ref), Pair(core_ref, lo_ref, lx_ref)
    a, b = a_ref[...], b_ref[...]
    s_p = product(inverse[0], joined(jnp.where(even, a, b)))
    cat = joined(s_p)
    s_q = product(inverse[1], joined(jnp.where(even, b, a) - stacked(core_ref, qo_ref, qx_ref, cat)))
    both_ways(even, -product(below[0], cat) - product(below[1], joined(s_q)), one_ref, two_ref)
    p_ref[...] = s_p
    q_ref[...] = s_q


def less_kernel(core_ref, even_ref, lo_ref, lx_ref, p_ref, q_ref, acc_ref, one_ref, two_ref):
    below = Pair(core_ref, lo_ref, lx_ref)
    part = product(below[0], joined(p_ref[...])) + product(below[1], joined(q_ref[...]))
    both_ways(even_ref[0] == 1, acc_ref[...] - part, one_ref, two_ref)


def merge_kernel(own_ref, x_ref, y_ref, mine_ref, out_ref):
    out_ref[...] = x_ref[...] + y_ref[...] + mine_ref[...] * own_ref[0].astype(F32)


def final_kernel(
    core_ref, even_ref, io_ref, ix_ref, qo_ref, qx_ref, a_ref, b_ref, c_ref, d_ref, *refs
):
    known, out_ref = refs[:-1], refs[-1]
    even = even_ref[0] == 1
    inverse = Pair(core_ref, io_ref, ix_ref)
    one, two = a_ref[...] + c_ref[...], b_ref[...] + d_ref[...]
    s_p = product(inverse[0], joined(unpacked(jnp.where(even, one, two))))
    rest = unpacked(jnp.where(even, two, one)) - stacked(core_ref, qo_ref, qx_ref, joined(s_p))
    s_q = product(inverse[1], joined(rest))
    n = s_p.shape[0] // 2
    for slot, s in ((0, s_p), (1, s_q)):
        old = functools.reduce(jnp.add, [k[...] for k in known[slot::2]])
        old = jnp.where(even, packed(old, 0), packed(old, 1))
        out_ref[slot] = old + jnp.concatenate([s[:n], s[n:]], axis=1)


def update_kernel(core_ref, keep_ref, o0_ref, x0_ref, o1_ref, x1_ref, s_ref, out_ref, solved_ref):
    parts, _, rows, width = out_ref.shape
    steps, cuts = s_ref.shape[0] // 2, s_ref.shape[1]
    for slot in range(2):
        sides = []
        for half in range(cuts):
            pieces = [s_ref[slot * steps + j, half] for j in range(steps)]
            sides.append(unpacked(jnp.concatenate(pieces, axis=0)))
        solved_ref[slot] = jnp.concatenate(sides, axis=1)
    cats = [joined(solved_ref[slot]) for slot in range(2)]
    for a, w in enumerate((Pair(core_ref, o0_ref, x0_ref), Pair(core_ref, o1_ref, x1_ref))):
        terms = [product(w[slot], cats[slot]) for slot in range(2)]
        if a == 0:
            terms = [t * keep_ref[slot] for slot, t in enumerate(terms)]
        total = terms[0] + terms[1]
        for j in range(parts):
            out_ref[j, a] = total[j * rows : (j + 1) * rows]


def shards(panel, right_side, inverse_blocks):
    block = panel.shape[2]
    width = right_side.shape[3] // 2
    my_row, my_col = lax.axis_index("row"), lax.axis_index("col")
    row_count, col_count = lax.axis_size("row"), lax.axis_size("col")
    planes = row_count // 2
    plane, core = my_row // 2, my_row % 2

    def flag(condition):
        return jnp.asarray(condition).astype(jnp.int32).reshape(1)

    core_arg, even, zero = flag(core), flag(my_col % 2 == 0), flag(False)
    not_3, own_flag = flag(my_col != 3), flag((plane == 3) & (my_col == 7))
    keep = (my_col > 2 * plane + jnp.arange(2)).astype(F32)
    root = jnp.where(plane == 3, 6, 2 * plane + 2)
    share = block // row_count
    first_column, first_row = core * width, my_row * share
    (panel, core_arg, even, zero, not_3, own_flag, keep, root, first_column, first_row) = lax.optimization_barrier(
        (panel, core_arg, even, zero, not_3, own_flag, keep, root, first_column, first_row)
    )
    whole = ((block, width), F32)
    slim = ((block // 2, width), F32)

    def send(array, moves):
        pairs = [
            ((2 * a + h) * col_count + b, (2 * c + h) * col_count + d)
            for (a, b), (c, d) in moves
            for h in range(2)
        ]
        return lax.ppermute(array, BOTH, pairs)

    def swap(array):
        return lax.ppermute(array, "row", [(r, r ^ 1) for r in range(row_count)])

    inverse = inverse_blocks[0]
    rhs = lax.dynamic_slice(right_side, (0, 0, 0, first_column), (1, 1, block, width)).reshape(block, width)
    near = send(rhs, [((0, 0), (0, 1)), ((1, 0), (0, 2)), ((3, 0), (0, 3))])
    tile = retile(after(panel, rhs), 0)
    inverses = (inverse, swap(inverse))
    belows = (tile, swap(tile))
    far = send(after(rhs, tile), [((z, 0), (0, 4 + z)) for z in range(4)])

    def solve_first(choice, a, b, c):
        specs = [SMEM] * 2 + [VMEM] * 7
        return call(first_kernel, "first", 2, [whole] * 2, specs, core_arg, choice, *inverses, *belows, a, b, c)

    def solve_second(r, u):
        return call(second_kernel, "second", 1, [whole], [SMEM] + [VMEM] * 4, core_arg, *inverses, r, u)[0]

    def subtract(acc, u, *parts):
        specs = [SMEM] + [VMEM] * (4 + len(parts))
        return call(third_kernel, "third", 1, [whole] * 2, specs, core_arg, *belows, acc, u, *parts)

    p_0, u = solve_first(zero, near, far, far)
    s_q = solve_second(rhs, u)
    to_2 = send(s_q, [((0, 1), (0, 2))])
    to_3 = send(s_q, [((0, 1), (0, 3))])

    half_shape = ((block // 2, block), F32)
    (ahead,) = call(cut_kernel, "cut", 0, [half_shape], [SMEM] + [VMEM] * 2, core_arg, tile, after(belows[1], s_q))
    x = send(ahead, [((2, 5), (2, 6)), ((3, 7), (3, 6))])
    y = send(ahead, [((2, 5), (2, 7))])

    soon, q_0 = subtract(rhs, u, after(to_2, ahead), to_3)
    a = send(soon, [((0, 2), (1, 3))])
    b = send(soon, [((0, 3), (1, 3)), ((0, 2), (1, 4))])
    c = send(soon, [((0, 2), (1, 5))])
    late_5 = send(after(s_q, soon), [((0, 1), (0, 5))])
    late_4 = send(after(s_q, soon), [((0, 1), (0, 4))])
    late_6 = send(q_0, [((0, 2), (0, 6)), ((0, 3), (0, 7))])
    later, _ = subtract(rhs, u, late_4, late_5, late_6)
    acc = send(later, [((0, c), (1, c)) for c in range(4, 8)])

    (got,) = call(
        merge_kernel, "merge", 0, [half_shape], [SMEM] + [VMEM] * 3, own_flag, after(x, soon), y, ahead
    )
    coupling = (got, swap(got))

    a = after(a, got)
    p_1, u = solve_first(not_3, a, b, c)
    s_q = solve_second(b, u)
    to_4 = send(s_q, [((1, 3), (1, 4))])
    to_5 = send(s_q, [((1, 3), (1, 5))])
    soon, q_1 = subtract(acc, u, to_4, to_5)
    a = send(soon, [((1, 4), (2, 6)), ((1, 5), (2, 7))])
    b = send(soon, [((1, 4), (2, 7)), ((1, 5), (2, 6))])
    late = [send(s, [((1, 4), (1, 6)), ((1, 5), (1, 7))]) for s in (p_1, q_1)]
    specs = [SMEM] * 2 + [VMEM] * 5
    one, two = call(less_kernel, "less", 2, [slim] * 2, specs, core_arg, even, *belows, *late, acc)
    c = send(one, [((1, 6), (3, 6)), ((1, 7), (3, 7))])
    d = send(two, [((1, 6), (3, 7)), ((1, 7), (3, 6))])

    specs = [SMEM] * 2 + [VMEM] * 8
    outs = [slim] * 2 + [whole] * 2
    one, two, p_2, q_2 = call(
        pair_kernel, "pair", 5, outs, specs, core_arg, even, *inverses, *belows, *coupling, a, b
    )
    a = send(one, [((2, 6), (3, 6)), ((2, 7), (3, 7))])
    b = send(two, [((2, 6), (3, 7)), ((2, 7), (3, 6))])

    specs = [SMEM] * 2 + [VMEM] * 14
    known = (p_0, q_0, p_1, q_1, p_2, q_2)
    outs = [((2, block // 2, width), F32)]
    (mine,) = call(
        final_kernel, "final", 3, outs, specs, core_arg, even, *inverses, *coupling, a, b, c, d, *known
    )

    tile = retile(after(panel, mine), 1)
    cut = block // col_count
    pieces = lax.all_to_all(mine.reshape(col_count, cut, width), "col", 0, 0)
    piece = lax.dynamic_slice_in_dim(pieces, root, 2, 0)
    pieces = lax.all_to_all(jnp.broadcast_to(piece[None], (col_count, 2, cut, width)), "col", 0, 0)

    outs = [((row_count, 2, share, width), F32), ((2, block, width), F32)]
    specs = [SMEM] * 2 + [VMEM] * 5
    parts, mine = call(update_kernel, "update", 4, outs, specs, core_arg, keep, *belows, tile, swap(tile), pieces)
    parts = lax.all_to_all(parts, "row", 0, 0)
    sums = parts.reshape(planes, 2, 2, share, width).sum(0)
    sums = jnp.concatenate([sums[0], sums[1]], axis=-1)
    own = lax.dynamic_slice_in_dim(right_side, first_row, share, 2).reshape(2, share, 2 * width)
    updated = (own - sums).reshape(2, 1, share, 2 * width)

    ours = jnp.where(core == 0, mine[0], mine[1])
    theirs = swap(jnp.where(core == 0, mine[1], mine[0]))
    solved = jnp.concatenate([jnp.where(core == 0, ours, theirs), jnp.where(core == 0, theirs, ours)], axis=1)
    return solved.reshape(1, block, 2 * width), updated


def solution(mesh):
    placed = (P(None, "col", None, "row", None), P(None, "col", None, None), P("row", None, None))
    return jax.shard_map(
        shards,
        mesh=mesh,
        in_specs=placed,
        out_specs=(P("row", None, None), P(None, "col", "row", None)),
        check_vma=False,
    )
```

time: 300 us -> 243 us (0.81)
  local copies, waits for them, and re-layouts: 51.8 us -> 10.5 us
  Pallas kernels: 62.3 us -> 44.1 us
  waiting for transfers between devices: 46.1 us -> 50.2 us
    unnamed x62 -> x14, local copies, waits for them, and re-layouts: 49 us -> 8.1 us
    all_to_all x1, starting transfers between devices: 33.3 us -> 48.5 us  [shards(): pieces = lax.all_to_all(mine.reshape(col_count, cut, width), 'col', 0, 0)]
    pallas_call x13, Pallas kernels: 44.6 us -> 34.8 us  [call(): pl.pallas_call(kernel, out_shape=tuple((jax.ShapeDtypeStruct(shape, kind)...]
    pallas_call x3 -> x0, Pallas kernels: 8.5 us -> none  [place(): pl.pallas_call(place_kernel, out_shape=[jax.ShapeDtypeStruct((2, 2, n, de...]
    ppermute x23, starting transfers between devices: 27.7 us -> 19.8 us  [send(): return lax.ppermute(array, BOTH, pairs)]
    all_to_all x1, starting transfers between devices: 60.9 us -> 53.9 us  [shards(): parts = lax.all_to_all(parts, 'row', 0, 0)]
  transfers between devices with their start and end apart: 31 -> 31, of which waited for: 5 -> 5; matrix products, arithmetic and copies ran while one was open for 1% -> 1% of each run, Pallas kernels for 11% -> 7%
where the time goes in v3:
time: 243 us; the launch traced here: 242 us
  starting transfers between devices  133 us (55%)
  waiting for transfers between devices  50.2 us (21%)
  Pallas kernels  44.1 us (18%)
  local copies, waits for them, and re-layouts  10.5 us (4%)
  other arithmetic  2.97 us (1%)
    all_to_all x1, starting transfers between devices, shards(): parts = lax.all_to_all(parts, 'row', 0, 0)  53.9 us
    all_to_all x1, starting transfers between devices, shards(): pieces = lax.all_to_all(mine.reshape(col_count, cut, width), 'col', 0, 0)  48.5 us
    pallas_call x13, Pallas kernels, call(): pl.pallas_call(kernel, out_shape=tuple((jax.ShapeDtypeStruct(shape, kind)...  34.8 us
    ppermute x23, starting transfers between devices, send(): return lax.ppermute(array, BOTH, pairs)  19.8 us
    all_to_all x1, waiting for transfers between devices, shards(): lax.all_to_all(jnp.broadcast_to(piece[None], (col_count, 2, cut, width)),...  15.2 us
    all_to_all x1, waiting for transfers between devices, shards(): parts = lax.all_to_all(parts, 'row', 0, 0)  14 us
    ppermute x23, waiting for transfers between devices, send(): return lax.ppermute(array, BOTH, pairs)  10.9 us
    all_to_all x1, waiting for transfers between devices, shards(): pieces = lax.all_to_all(mine.reshape(col_count, cut, width), 'col', 0, 0)  10.1 us
  transfers between devices with their start and end apart: 31, of which 5 were waited for; matrix products, arithmetic and copies ran while one was open for 1% of the time, Pallas kernels for 7%

profile of v3, /device:TPU:1, one launch (start us, length us, event | category | flops | bytes accessed | tf_op | source)
XLA Modules:
  0.0 241.9 jit_solution(9921217173591371250)
XLA Ops:
  0.7 1.2 dynamic-slice_bitcast_fusion.r_ref.acc_ref
  2.0 4.3 %retile.2.lo_ref.own_ref.o0_ref = f32[1024,1024]{1,0:T(8,128)} custom-call(f32[2,1,1024,1,1024]{4,3,2,1,0:T(1,128)} %panel_ref.1), custom_call_target="tpu_custom_call" | custom-call | bytes 8388608 | tf_op jit(solution)/shard_map/retile/pallas_call | solution.py:91
  6.3 1.7 collective-permute-start
  8.1 3.2 %collective-permute-start.3 = (f32[1024,128]{1,0:T(8,128)S(1)}, f32[1024,128]{1,0:T(8,128)S(1)}, u32[]{:S(2)}, u32[]{:S(2)}) collective-permute-start(f32[1024,128]{1,0:T(8,128)S(1)} %dynamic-slice_bitcast_fusion.r_ref.acc_ref), channel_id=1, source_target_pairs={{0,4},{16,20},{32,5},{48,21},{64,6},{80,22},{96,7},{112,23}} | collective-permute-start | bytes 1572872 | tf_op jit(solution)/shard_map/ppermute | solution.py:228
  11.3 1.3 collective-permute-start.2
  12.6 9.5 %collective-permute-done.3.b_ref.c_ref = f32[1024,128]{1,0:T(8,128)S(1)} collective-permute-done((f32[1024,128]{1,0:T(8,128)S(1)}, f32[1024,128]{1,0:T(8,128)S(1)}, u32[]{:S(2)}, u32[]{:S(2)}) %collective-permute-start.3) | collective-permute-done | bytes 524320 | tf_op jit(solution)/shard_map/ppermute | solution.py:228
  22.1 1.3 collective-permute-done.2.a_ref
  23.5 3.7 %copy-done = f32[1024,1024]{1,0:T(8,128)S(1)} copy-done((f32[1024,1024]{1,0:T(8,128)S(1)}, f32[1024,1024]{1,0:T(8,128)}, u32[]{:S(2)}) %copy-start) | copy-done | bytes 4194328
  27.2 2.4 first.2
  29.6 1.3 second.2
  34.1 1.3 third.3
  37.8 1.3 collective-permute-start.8
  41.3 1.6 third.4
  43.8 2.4 %first.3 = (f32[1024,128]{1,0:T(8,128)S(1)}, f32[1024,128]{1,0:T(8,128)S(1)}) custom-call(s32[1]{0:T(128)} %bitcast.core_ref, s32[1]{0:T(128)} %bitcast.2.flag_ref, f32[1024,1024]{1,0:T(8,128)S(1)} %bitcast.25, f32[1024,1024]{1,0:T(8,128)S(1)} %collective-permute-done.1.ix_ref, f32[1024,1024]{1,0:T(8,128)S(1)} %copy-done, ...), custom_call_target="tpu_custom_call" | custom-call | flops 1610612736 | bytes 8388608 | tf_op jit(solution)/shard_map/first/pallas_call | solution.py:68
  46.2 1.3 second.3
  49.7 1.3 third.5
  53.1 2.4 %less.1 = (f32[512,128]{1,0:T(8,128)S(1)}, f32[512,128]{1,0:T(8,128)S(1)}) custom-call(s32[1]{0:T(128)} %bitcast.core_ref, s32[1]{0:T(128)} %bitcast.1.even_ref, f32[1024,1024]{1,0:T(8,128)S(1)} %copy-done, f32[1024,1024]{1,0:T(8,128)S(1)} %collective-permute-done.lx_ref.other_ref.x0_ref, f32[1024,128]{1,0:T(8,128)S(1)} %collective-permute-done.22.p_ref, ...), custom_call_target="tpu_custom_call" | custom-call | flops 1610612736 | bytes 8388608 | tf_op jit(solution)/shard_map/less/pallas_call | solution.py:68
  57.3 6.0 %pair.1 = (f32[512,128]{1,0:T(8,128)S(1)}, f32[512,128]{1,0:T(8,128)S(1)}, f32[1024,128]{1,0:T(8,128)S(1)}, f32[1024,128]{1,0:T(8,128)S(1)}) custom-call(s32[1]{0:T(128)} %bitcast.core_ref, s32[1]{0:T(128)} %bitcast.1.even_ref, f32[1024,1024]{1,0:T(8,128)S(1)} %bitcast.27, f32[1024,1024]{1,0:T(8,128)S(1)} %collective-permute-done.1.ix_ref, ...), custom_call_target="tpu_custom_call" | custom-call | flops 4026531840 | bytes 20971520 | tf_op jit(solution)/shard_map/pair/pallas_call | solution.py:68
  64.7 5.1 %final.1 = f32[2,512,128]{2,1,0:T(8,128)} custom-call(s32[1]{0:T(128)} %bitcast.core_ref, s32[1]{0:T(128)} %bitcast.1.even_ref, f32[1024,1024]{1,0:T(8,128)S(1)} %bitcast.28, f32[1024,1024]{1,0:T(8,128)S(1)} %collective-permute-done.1.ix_ref, f32[512,1024]{1,0:T(8,128)S(1)} %merge.1.qo_ref, f32[512,1024]{1,0:T(8,128)S(1)} %collective-permute-done.8.qx_ref, ...), custom_call_target="tpu_custom_call" | custom-call | flops 2415919104 | bytes 12582912 | tf_op jit(solution)/shard_map/final/pallas_call | solution.py:68
  69.8 5.0 %retile.3.o1_ref = f32[1024,1024]{1,0:T(8,128)} custom-call(f32[2,1,1024,1,1024]{4,3,2,1,0:T(1,128)S(1)} %bitcast.30), custom_call_target="tpu_custom_call" | custom-call | bytes 8388608 | tf_op jit(solution)/shard_map/retile/pallas_call | solution.py:91
  74.9 48.5 %all-to-all-start = ((f32[16,64,128]{2,1,0:T(8,128)}), f32[16,64,128]{2,1,0:T(8,128)S(1)}, u32[]{:S(2)}, u32[]{:S(2)}) async-start(f32[16,64,128]{2,1,0:T(8,128)} %bitcast.6), calls=%async_computation | async-start | bytes 1048576 | tf_op jit(solution)/shard_map/all_to_all | solution.py:308
  123.5 10.1 %all-to-all-done = f32[16,64,128]{2,1,0:T(8,128)S(1)} async-done(((f32[16,64,128]{2,1,0:T(8,128)}), f32[16,64,128]{2,1,0:T(8,128)S(1)}, u32[]{:S(2)}, u32[]{:S(2)}) %all-to-all-start) | async-done | bytes 524320 | tf_op jit(solution)/shard_map/all_to_all | solution.py:308
  133.6 1.1 broadcast_in_dim.2
  134.7 4.4 %all-to-all-start.1 = ((f32[16,2,64,128]{3,2,1,0:T(8,128)}), f32[16,2,64,128]{3,2,1,0:T(8,128)S(1)}, u32[]{:S(2)}, u32[]{:S(2)}) async-start(f32[16,2,64,128]{3,2,1,0:T(8,128)} %broadcast_in_dim.2), calls=%async_computation.1 | async-start | bytes 2097152 | tf_op jit(solution)/shard_map/all_to_all | solution.py:310
  139.1 15.2 %all-to-all-done.1.s_ref = f32[16,2,64,128]{3,2,1,0:T(8,128)S(1)} async-done(((f32[16,2,64,128]{3,2,1,0:T(8,128)}), f32[16,2,64,128]{3,2,1,0:T(8,128)S(1)}, u32[]{:S(2)}, u32[]{:S(2)}) %all-to-all-start.1) | async-done | bytes 1048608 | tf_op jit(solution)/shard_map/all_to_all | solution.py:310
  154.3 2.2 copy-done.1
  156.5 2.2 copy-done.3
  158.7 9.2 %update.1 = (f32[8,2,128,128]{3,2,1,0:T(8,128)}, f32[2,1024,128]{2,1,0:T(8,128)S(1)}) custom-call(s32[1]{0:T(128)} %bitcast.core_ref, f32[2]{0:T(128)S(1)} %compare_convert_fusion.keep_ref, f32[1024,1024]{1,0:T(8,128)S(1)} %copy-done.1, f32[1024,1024]{1,0:T(8,128)S(1)} %copy-done.3, f32[1024,1024]{1,0:T(8,128)} %retile.3.o1_ref, ...), custom_call_target="tpu_custom_call" | custom-call | flops 3221225472 | bytes 16777216 | tf_op jit(solution)/shard_map/update/pallas_call | solution.py:68
  167.9 3.2 %collective-permute-start.27 = (f32[1024,128]{1,0:T(8,128)S(1)}, f32[1024,128]{1,0:T(8,128)S(1)}, u32[]{:S(2)}, u32[]{:S(2)}) collective-permute-start(f32[1024,128]{1,0:T(8,128)S(1)} %select_bitcast_fusion), channel_id=1, source_target_pairs={{0,16},{16,0},{32,48},{48,32},{64,80},{80,64},{96,112},{112,96},{1... | collective-permute-start | bytes 1572872 | tf_op jit(solution)/shard_map/ppermute | solution.py:231
  171.1 53.9 %all-to-all-start.2 = ((f32[8,2,128,128]{3,2,1,0:T(8,128)}), f32[8,2,128,128]{3,2,1,0:T(8,128)S(1)}, u32[]{:S(2)}, u32[]{:S(2)}) async-start(f32[8,2,128,128]{3,2,1,0:T(8,128)} %get-tuple-element.71), calls=%async_computation.2 | async-start | bytes 2097152 | tf_op jit(solution)/shard_map/all_to_all | solution.py:315
  226.1 14.0 %all-to-all-done.2 = f32[8,2,128,128]{3,2,1,0:T(8,128)S(1)} async-done(((f32[8,2,128,128]{3,2,1,0:T(8,128)}), f32[8,2,128,128]{3,2,1,0:T(8,128)S(1)}, u32[]{:S(2)}, u32[]{:S(2)}) %all-to-all-start.2) | async-done | bytes 1048608 | tf_op jit(solution)/shard_map/all_to_all | solution.py:315
  240.2 1.7 maximum_subtract_fusion
  (70 shorter events, 17.3 us)
Async XLA Ops:
  6.3 17.2 %collective-permute-start = (f32[1024,1024]{1,0:T(8,128)}, f32[1024,1024]{1,0:T(8,128)S(1)}, u32[]{:S(2)}, u32[]{:S(2)}) collective-permute-start(f32[1024,1024]{1,0:T(8,128)} %retile.2.lo_ref.own_ref.o0_ref), channel_id=1, source_target_pairs={{0,16},{16,0},{32,48},{48,32},{64,80},{80,64},{96,112},{112,96},{1... | collective-permute-start | bytes 12582920 | tf_op jit(solution)/shard_map/ppermute | solution.py:231
  8.0 15.5 %collective-permute-start.1 = (f32[1024,1024]{1,0:T(8,128)S(1)}, f32[1024,1024]{1,0:T(8,128)S(1)}, u32[]{:S(2)}, u32[]{:S(2)}) collective-permute-start(f32[1024,1024]{1,0:T(8,128)S(1)} %bitcast.22), channel_id=1, source_target_pairs={{0,16},{16,0},{32,48},{48,32},{64,80},{80,64},{96,112},{112,96},{1... | collective-permute-start | bytes 12582920 | tf_op jit(solution)/shard_map/ppermute | solution.py:231
  8.1 14.1 %collective-permute-start.3 = (f32[1024,128]{1,0:T(8,128)S(1)}, f32[1024,128]{1,0:T(8,128)S(1)}, u32[]{:S(2)}, u32[]{:S(2)}) collective-permute-start(f32[1024,128]{1,0:T(8,128)S(1)} %dynamic-slice_bitcast_fusion.r_ref.acc_ref), channel_id=1, source_target_pairs={{0,4},{16,20},{32,5},{48,21},{64,6},{80,22},{96,7},{112,23}} | collective-permute-start | bytes 1572872 | tf_op jit(solution)/shard_map/ppermute | solution.py:228
  11.3 12.2 %collective-permute-start.2 = (f32[1024,128]{1,0:T(8,128)S(1)}, f32[1024,128]{1,0:T(8,128)S(1)}, u32[]{:S(2)}, u32[]{:S(2)}) collective-permute-start(f32[1024,128]{1,0:T(8,128)S(1)} %dynamic-slice_bitcast_fusion.r_ref.acc_ref), channel_id=1, source_target_pairs={{0,1},{16,17},{32,2},{48,18},{96,3},{112,19}} | collective-permute-start | bytes 1572872 | tf_op jit(solution)/shard_map/ppermute | solution.py:228
  23.5 33.9 %copy-start.2 = (f32[1024,1024]{1,0:T(8,128)}, f32[1024,1024]{1,0:T(8,128)S(1)}, u32[]{:S(2)}) copy-start(f32[1024,1024]{1,0:T(8,128)S(1)} %collective-permute-done.lx_ref.other_ref.x0_ref) | copy-start | bytes 12582916
  31.1 6.4 %collective-permute-start.4 = (f32[512,1024]{1,0:T(8,128)S(1)}, f32[512,1024]{1,0:T(8,128)S(1)}, u32[]{:S(2)}, u32[]{:S(2)}) collective-permute-start(f32[512,1024]{1,0:T(8,128)S(1)} %cut.1.mine_ref), channel_id=1, source_target_pairs={{69,70},{85,86},{103,102},{119,118}} | collective-permute-start | bytes 6291464 | tf_op jit(solution)/shard_map/ppermute | solution.py:228
  31.9 5.7 %collective-permute-start.7 = (f32[512,1024]{1,0:T(8,128)S(1)}, f32[512,1024]{1,0:T(8,128)S(1)}, u32[]{:S(2)}, u32[]{:S(2)}) collective-permute-start(f32[512,1024]{1,0:T(8,128)S(1)} %cut.1.mine_ref), channel_id=1, source_target_pairs={{69,71},{85,87}} | collective-permute-start | bytes 6291464 | tf_op jit(solution)/shard_map/ppermute | solution.py:228
  32.7 1.4 collective-permute-start.5
  33.4 0.7 collective-permute-start.6
  35.4 4.5 %collective-permute-start.10 = (f32[1024,128]{1,0:T(8,128)S(1)}, f32[1024,128]{1,0:T(8,128)S(1)}, u32[]{:S(2)}, u32[]{:S(2)}) collective-permute-start(f32[1024,128]{1,0:T(8,128)S(1)} %second.2), channel_id=1, source_target_pairs={{1,5},{17,21}} | collective-permute-start | bytes 1572872 | tf_op jit(solution)/shard_map/ppermute | solution.py:228
  36.1 4.5 %collective-permute-start.9 = (f32[1024,128]{1,0:T(8,128)S(1)}, f32[1024,128]{1,0:T(8,128)S(1)}, u32[]{:S(2)}, u32[]{:S(2)}) collective-permute-start(f32[1024,128]{1,0:T(8,128)S(1)} %second.2), channel_id=1, source_target_pairs={{1,4},{17,20}} | collective-permute-start | bytes 1572872 | tf_op jit(solution)/shard_map/ppermute | solution.py:228
  36.8 4.5 %collective-permute-start.11 = (f32[1024,128]{1,0:T(8,128)S(1)}, f32[1024,128]{1,0:T(8,128)S(1)}, u32[]{:S(2)}, u32[]{:S(2)}) collective-permute-start(f32[1024,128]{1,0:T(8,128)S(1)} %get-tuple-element.52.refs_1_), channel_id=1, source_target_pairs={{2,6},{18,22},{3,7},{19,23}} | collective-permute-start | bytes 1572872 | tf_op jit(solution)/shard_map/ppermute | solution.py:228
  37.8 19.5 %collective-permute-start.8 = (f32[512,1024]{1,0:T(8,128)S(1)}, f32[512,1024]{1,0:T(8,128)S(1)}, u32[]{:S(2)}, u32[]{:S(2)}) collective-permute-start(f32[512,1024]{1,0:T(8,128)S(1)} %merge.1.qo_ref), channel_id=1, source_target_pairs={{0,16},{16,0},{32,48},{48,32},{64,80},{80,64},{96,112},{112,96},{1... | collective-permute-start | bytes 6291464 | tf_op jit(solution)/shard_map/ppermute | solution.py:231
  39.2 4.6 %collective-permute-start.13 = (f32[1024,128]{1,0:T(8,128)S(1)}, f32[1024,128]{1,0:T(8,128)S(1)}, u32[]{:S(2)}, u32[]{:S(2)}) collective-permute-start(f32[1024,128]{1,0:T(8,128)S(1)} %get-tuple-element.49), channel_id=1, source_target_pairs={{2,35},{18,51}} | collective-permute-start | bytes 1572872 | tf_op jit(solution)/shard_map/ppermute | solution.py:228
  39.9 3.9 %collective-permute-start.14 = (f32[1024,128]{1,0:T(8,128)S(1)}, f32[1024,128]{1,0:T(8,128)S(1)}, u32[]{:S(2)}, u32[]{:S(2)}) collective-permute-start(f32[1024,128]{1,0:T(8,128)S(1)} %get-tuple-element.49), channel_id=1, source_target_pairs={{3,35},{19,51},{2,36},{18,52}} | collective-permute-start | bytes 1572872 | tf_op jit(solution)/shard_map/ppermute | solution.py:228
  40.6 3.2 %collective-permute-start.15 = (f32[1024,128]{1,0:T(8,128)S(1)}, f32[1024,128]{1,0:T(8,128)S(1)}, u32[]{:S(2)}, u32[]{:S(2)}) collective-permute-start(f32[1024,128]{1,0:T(8,128)S(1)} %get-tuple-element.49), channel_id=1, source_target_pairs={{2,37},{18,53}} | collective-permute-start | bytes 1572872 | tf_op jit(solution)/shard_map/ppermute | solution.py:228
  42.9 6.7 %collective-permute-start.12 = (f32[1024,128]{1,0:T(8,128)S(1)}, f32[1024,128]{1,0:T(8,128)S(1)}, u32[]{:S(2)}, u32[]{:S(2)}) collective-permute-start(f32[1024,128]{1,0:T(8,128)S(1)} %get-tuple-element.53), channel_id=1, source_target_pairs={{4,36},{20,52},{5,37},{21,53},{6,38},{22,54},{7,39},{23,55}} | collective-permute-start | bytes 1572872 | tf_op jit(solution)/shard_map/ppermute | solution.py:228
  47.5 2.1 collective-permute-start.16
  48.2 1.4 collective-permute-start.17
  48.9 4.1 %collective-permute-start.22 = (f32[1024,128]{1,0:T(8,128)S(1)}, f32[1024,128]{1,0:T(8,128)S(1)}, u32[]{:S(2)}, u32[]{:S(2)}) collective-permute-start(f32[1024,128]{1,0:T(8,128)S(1)} %get-tuple-element.60.refs_2_), channel_id=1, source_target_pairs={{36,38},{52,54},{37,39},{53,55}} | collective-permute-start | bytes 1572872 | tf_op jit(solution)/shard_map/ppermute | solution.py:228
  51.0 2.1 collective-permute-start.23
  51.7 5.6 %collective-permute-start.18 = (f32[1024,128]{1,0:T(8,128)S(1)}, f32[1024,128]{1,0:T(8,128)S(1)}, u32[]{:S(2)}, u32[]{:S(2)}) collective-permute-start(f32[1024,128]{1,0:T(8,128)S(1)} %get-tuple-element.57), channel_id=1, source_target_pairs={{36,70},{52,86},{37,71},{53,87}} | collective-permute-start | bytes 1572872 | tf_op jit(solution)/shard_map/ppermute | solution.py:228
  52.4 4.9 %collective-permute-start.19 = (f32[1024,128]{1,0:T(8,128)S(1)}, f32[1024,128]{1,0:T(8,128)S(1)}, u32[]{:S(2)}, u32[]{:S(2)}) collective-permute-start(f32[1024,128]{1,0:T(8,128)S(1)} %get-tuple-element.57), channel_id=1, source_target_pairs={{36,71},{52,87},{37,70},{53,86}} | collective-permute-start | bytes 1572872 | tf_op jit(solution)/shard_map/ppermute | solution.py:228
  55.6 9.2 %collective-permute-start.24 = (f32[512,128]{1,0:T(8,128)S(1)}, f32[512,128]{1,0:T(8,128)S(1)}, u32[]{:S(2)}, u32[]{:S(2)}) collective-permute-start(f32[512,128]{1,0:T(8,128)S(1)} %get-tuple-element.62), channel_id=1, source_target_pairs={{38,102},{54,118},{39,103},{55,119}} | collective-permute-start | bytes 786440 | tf_op jit(solution)/shard_map/ppermute | solution.py:228
  56.3 8.5 %collective-permute-start.25 = (f32[512,128]{1,0:T(8,128)S(1)}, f32[512,128]{1,0:T(8,128)S(1)}, u32[]{:S(2)}, u32[]{:S(2)}) collective-permute-start(f32[512,128]{1,0:T(8,128)S(1)} %get-tuple-element.63), channel_id=1, source_target_pairs={{38,103},{54,119},{39,102},{55,118}} | collective-permute-start | bytes 786440 | tf_op jit(solution)/shard_map/ppermute | solution.py:228
  63.3 1.4 collective-permute-start.20
  64.0 0.7 collective-permute-start.21
  74.8 79.5 %collective-permute-start.26 = (f32[1024,1024]{1,0:T(8,128)}, f32[1024,1024]{1,0:T(8,128)}, u32[]{:S(2)}, u32[]{:S(2)}) collective-permute-start(f32[1024,1024]{1,0:T(8,128)} %retile.3.o1_ref), channel_id=1, source_target_pairs={{0,16},{16,0},{32,48},{48,32},{64,80},{80,64},{96,112},{112,96},{1... | collective-permute-start | bytes 12582920 | tf_op jit(solution)/shard_map/ppermute | solution.py:231
  74.9 58.7 %all-to-all-start = ((f32[16,64,128]{2,1,0:T(8,128)}), f32[16,64,128]{2,1,0:T(8,128)S(1)}, u32[]{:S(2)}, u32[]{:S(2)}) async-start(f32[16,64,128]{2,1,0:T(8,128)} %bitcast.6), calls=%async_computation | async-start | bytes 1048576 | tf_op jit(solution)/shard_map/all_to_all | solution.py:308
  134.7 19.6 %all-to-all-start.1 = ((f32[16,2,64,128]{3,2,1,0:T(8,128)}), f32[16,2,64,128]{3,2,1,0:T(8,128)S(1)}, u32[]{:S(2)}, u32[]{:S(2)}) async-start(f32[16,2,64,128]{3,2,1,0:T(8,128)} %broadcast_in_dim.2), calls=%async_computation.1 | async-start | bytes 2097152 | tf_op jit(solution)/shard_map/all_to_all | solution.py:310
  167.9 57.1 %collective-permute-start.27 = (f32[1024,128]{1,0:T(8,128)S(1)}, f32[1024,128]{1,0:T(8,128)S(1)}, u32[]{:S(2)}, u32[]{:S(2)}) collective-permute-start(f32[1024,128]{1,0:T(8,128)S(1)} %select_bitcast_fusion), channel_id=1, source_target_pairs={{0,16},{16,0},{32,48},{48,32},{64,80},{80,64},{96,112},{112,96},{1... | collective-permute-start | bytes 1572872 | tf_op jit(solution)/shard_map/ppermute | solution.py:231
  171.1 69.0 %all-to-all-start.2 = ((f32[8,2,128,128]{3,2,1,0:T(8,128)}), f32[8,2,128,128]{3,2,1,0:T(8,128)S(1)}, u32[]{:S(2)}, u32[]{:S(2)}) async-start(f32[8,2,128,128]{3,2,1,0:T(8,128)} %get-tuple-element.71), calls=%async_computation.2 | async-start | bytes 2097152 | tf_op jit(solution)/shard_map/all_to_all | solution.py:315
  (6 other events, 44.4 us)
